TPU v7x, 32 devices: a whole 2x2x4 slice. The times are simulated.
32 devices in a mesh: dp: 8 (over z, x), blk: 4 (over y, core).
Axes of the slice: x: 2, y: 2, z: 4, core: 2. Of those that a mesh axis runs over, the one named last changes fastest.
Arguments:
- tokens: bfloat16 [1024, 16384], P('dp', 'blk'), may hold values from -6 to 6
- up_first: bfloat16 [128, 128, 128], P('blk', 'dp'), may hold values from -0.5 to 0.5
- up_second: bfloat16 [128, 128, 256], P('blk', 'dp'), may hold values from -0.5 to 0.5
- down_first: bfloat16 [128, 256, 128], P('blk', 'dp'), may hold values from -0.375 to 0.375
- down_second: bfloat16 [128, 128, 128], P('blk', 'dp'), may hold values from -0.5 to 0.5
- cotangent: bfloat16 [1024, 16384], P('dp', 'blk'), may hold values from -6 to 6
Outputs:
- input_grad: bfloat16 [1024, 16384], P('dp', 'blk')
- up_first_grad: float32 [128, 128, 128], P('blk')
- up_second_grad: float32 [128, 128, 256], P('blk', 'dp')
- down_first_grad: float32 [128, 256, 128], P('blk', 'dp')
- down_second_grad: float32 [128, 128, 128], P('blk')
All inputs are finite; a program needn't handle non-finite values.
Results may differ from a plain program's by a relative error of at most 0.0069.
Values may be sent and summed in bfloat16 or wider, within the bound.
A program may use at most 128 MiB of HBM per device.

v0:
```python
import math

import jax
import jax.numpy as jnp
from jax import lax
from jax.sharding import PartitionSpec as P


def activation(values):
    return jax.nn.gelu(values, approximate=True)


def permute_forward(lower, second):

    def apply_second(piece):
        if second is None:
            return (piece,)
        product = jnp.einsum("tbj,jbk->tjk", piece, second, preferred_element_type=jnp.float32)
        return (piece, product)

    return apply_second(lax.all_to_all(lower, "blk", split_axis=2, concat_axis=1, tiled=True))


def permute_backward(grad_out, second):
    spread = jnp.einsum(
        "tjk,jbk->tbj", grad_out, second, preferred_element_type=jnp.float32
    ).astype(jnp.bfloat16)
    return lax.all_to_all(spread, "blk", split_axis=1, concat_axis=2, tiled=True)


def per_device(tokens, up_first, up_second, down_first, down_second, cotangent):
    tok_rows = tokens.shape[0]
    local_blocks = up_first.shape[0]
    block_size = up_first.shape[2]
    factor = 1.0 / math.sqrt(tok_rows * lax.axis_size("dp"))
    gathered = (
        lax.all_gather(up_first, "dp", axis=1, tiled=True),
        lax.all_gather(up_second, "dp", axis=1, tiled=True),
        lax.all_gather(down_first, "dp", axis=1, tiled=True),
        lax.all_gather(down_second, "dp", axis=1, tiled=True),
    )
    full_uf, full_us, full_df, full_ds = gathered
    inputs_b = tokens.reshape(tok_rows, local_blocks, block_size)
    first_up = jnp.einsum(
        "tbi,bij->tbj", inputs_b, full_uf, preferred_element_type=jnp.float32
    ).astype(jnp.bfloat16)
    moved_up, pre_act = permute_forward(first_up, full_us)
    hidden = activation(pre_act).astype(jnp.bfloat16)
    first_down = jnp.einsum(
        "tbi,bij->tbj", hidden, full_df, preferred_element_type=jnp.float32
    ).astype(jnp.bfloat16)
    moved_down = permute_forward(first_down, None)[0]
    upstream = cotangent.reshape(tok_rows, local_blocks, block_size)
    grad_ds = jnp.einsum("tbj,tjk->jbk", moved_down, upstream, preferred_element_type=jnp.float32)
    back_down = permute_backward(upstream, full_ds)
    grad_df = jnp.einsum("tbi,tbj->bij", hidden, back_down, preferred_element_type=jnp.float32)
    hidden_grad = jnp.einsum("tbj,bij->tbi", back_down, full_df, preferred_element_type=jnp.float32)
    _, pull_back = jax.vjp(activation, pre_act)
    pre_grad = pull_back(hidden_grad)[0].astype(jnp.bfloat16)
    grad_us = jnp.einsum("tbj,tjk->jbk", moved_up, pre_grad, preferred_element_type=jnp.float32)
    back_up = permute_backward(pre_grad, full_us)
    grad_uf = jnp.einsum("tbi,tbj->bij", inputs_b, back_up, preferred_element_type=jnp.float32)
    input_grad = jnp.einsum(
        "tbj,bij->tbi", back_up, full_uf, preferred_element_type=jnp.float32
    ).astype(jnp.bfloat16)
    input_grad = input_grad.reshape(tok_rows, local_blocks * block_size)
    wide_sum = (
        lax.psum_scatter(grad_us, "dp", scatter_dimension=1, tiled=True),
        lax.psum_scatter(grad_df, "dp", scatter_dimension=1, tiled=True),
    )
    square_sum = lax.psum((grad_uf, grad_ds), "dp")
    grad_us = wide_sum[0] * factor
    grad_df = wide_sum[1] * factor
    grad_uf = square_sum[0] * factor
    grad_ds = square_sum[1] * factor
    return (input_grad, grad_uf, grad_us, grad_df, grad_ds)


def solution(mesh):
    placed = (
        P("dp", "blk"),
        P("blk", "dp", None),
        P("blk", "dp", None),
        P("blk", "dp", None),
        P("blk", "dp", None),
        P("dp", "blk"),
    )
    return jax.shard_map(
        per_device,
        mesh=mesh,
        in_specs=placed,
        out_specs=(
            P("dp", "blk"),
            P("blk", None, None),
            P("blk", "dp", None),
            P("blk", "dp", None),
            P("blk", None, None),
        ),
        check_vma=False,
    )
```

profile of v0, /device:TPU:0, one launch (start us, length us, event | category | flops | bytes accessed | tf_op | source)
XLA Modules:
  0.0 594.3 jit_solution(2437143320594861501)
XLA Ops:
  10.0 42.4 %all-gather.5.cloned.1.call-done = bf16[32,128,128]{2,1,0:T(8,128)(2,1)} async-done(((bf16[32,16,128]{2,1,0:T(8,128)(2,1)}), bf16[32,128,128]{2,1,0:T(8,128)(2,1)}) %all-gather.5.cloned.1.call-update) | async-done | bytes 1048592 | tf_op jit(solution)/shard_map/all_gather | solution.py:40
  52.3 2.4 fusion.11
  56.4 3.5 all-to-all-start
  59.9 32.9 %all-gather.9.cloned.1.call-done = bf16[32,128,128]{2,1,0:T(8,128)(2,1)} async-done(((bf16[32,16,128]{2,1,0:T(8,128)(2,1)}), bf16[32,128,128]{2,1,0:T(8,128)(2,1)}) %all-gather.9.cloned.1.call-update) | async-done | bytes 1048592 | tf_op jit(solution)/shard_map/all_gather | solution.py:37
  96.6 3.5 all-to-all-start.1
  101.3 13.3 %all-to-all-done.1 = bf16[128,32,128]{0,1,2:T(8,128)(2,1)S(1)} async-done(((bf16[128,32,128]{0,1,2:T(8,128)(2,1)}), bf16[128,32,128]{0,1,2:T(8,128)(2,1)S(1)}, u32[]{:S(2)}, u32[]{:S(2)}) %all-to-all-start.1) | async-done | bytes 1048608 | tf_op jit(solution)/shard_map/all_to_all | solution.py:21
  115.0 29.7 %all-gather.11.cloned.1.call-done = bf16[32,128,256]{2,1,0:T(8,128)(2,1)} async-done(((bf16[32,16,256]{2,1,0:T(8,128)(2,1)}), bf16[32,128,256]{2,1,0:T(8,128)(2,1)}) %all-gather.11.cloned.1.call-update) | async-done | bytes 2097168 | tf_op jit(solution)/shard_map/all_gather | solution.py:38
  144.7 4.4 fusion.24
  149.1 46.8 %all-gather.7.cloned.1.call-done = bf16[32,256,128]{2,1,0:T(8,128)(2,1)} async-done(((bf16[32,32,128]{2,1,0:T(8,128)(2,1)}), bf16[32,256,128]{2,1,0:T(8,128)(2,1)}) %all-gather.7.cloned.1.call-update) | async-done | bytes 2097168 | tf_op jit(solution)/shard_map/all_gather | solution.py:39
  195.9 5.3 fusion.14
  201.2 2.7 copy.83
  203.9 4.3 all-to-all-start.3
  208.2 6.1 %fusion.6 = bf16[128,32,256]{2,0,1:T(8,128)(2,1)S(1)} fusion(f32[32,128,256]{2,1,0:T(8,128)} %fusion.24, bf16[128,32,128]{0,2,1:T(8,128)(2,1)S(1)} %bitcast.105, bf16[32,256,128]{2,1,0:T(8,128)(2,1)} %all-gather.7.cloned.1.call-done), kind=kOutput, calls=%fused_computation.8 | convolution fusion | flops 289406976 | bytes 9437184 | tf_op jit(solution)/shard_map/tbj,bij->tbi/dot_general | solution.py:57
  218.1 4.7 all-to-all-done.3
  222.7 3.5 all-to-all-start.2
  228.8 11.9 %all-to-all-done.2 = bf16[128,128,32]{0,2,1:T(8,128)(2,1)S(1)} async-done(((bf16[128,128,32]{0,2,1:T(8,128)(2,1)}), bf16[128,128,32]{0,2,1:T(8,128)(2,1)S(1)}, u32[]{:S(2)}, u32[]{:S(2)}) %all-to-all-start.2) | async-done | bytes 1048608 | tf_op jit(solution)/shard_map/all_to_all | solution.py:28
  244.9 3.4 fusion.17
  248.4 6.1 %fusion.29 = f32[32,256,128]{2,1,0:T(8,128)} fusion(bf16[128,32,128]{0,2,1:T(8,128)(2,1)} %bitcast.104, f32[32,128,256]{2,1,0:T(8,128)} %fusion.24), kind=kOutput, calls=%fused_computation.43 | convolution fusion | flops 277872640 | bytes 9437184 | tf_op jit(solution)/shard_map/tbi,tbj->bij/dot_general | solution.py:56
  254.5 4.4 fusion.26
  263.8 138.6 %all-reduce.3.cloned.1.call-done = (f32[32,128,128]{1,2,0:T(8,128)}, f32[32,128,128]{1,2,0:T(8,128)}) async-done(((f32[32,128,128]{1,2,0:T(8,128)}, f32[32,128,128]{1,2,0:T(8,128)}), (f32[32,128,128]{1,2,0:T(8,128)}, f32[32,128,128]{1,2,0:T(8,128)})) %all-reduce.3.cloned.1.call-update) | async-done | bytes 4194320 | tf_op jit(solution)/shard_map/psum | solution.py:71
  402.4 4.0 broadcast_multiply_fusion
  406.4 2.9 copy.90
  411.1 82.1 %reduce-scatter.5.cloned.1.call-done = f32[32,32,128]{2,1,0:T(8,128)} async-done(((f32[32,256,128]{2,1,0:T(8,128)}), f32[32,32,128]{2,1,0:T(8,128)}) %reduce-scatter.5.cloned.1.call-update) | async-done | bytes 524304 | tf_op jit(solution)/shard_map/reduce_scatter | solution.py:69
  495.1 90.4 %reduce-scatter.3.cloned.1.call-done = f32[32,16,256]{2,1,0:T(8,128)} async-done(((f32[32,128,256]{2,1,0:T(8,128)}), f32[32,16,256]{2,1,0:T(8,128)}) %reduce-scatter.3.cloned.1.call-update) | async-done | bytes 524304 | tf_op jit(solution)/shard_map/reduce_scatter | solution.py:68
  (44 shorter events, 30.7 us)
Async XLA Ops:
  7.2 85.7 %copy-start = (bf16[128,4096]{1,0:T(8,128)(2,1)S(1)}, bf16[128,4096]{1,0:T(8,128)(2,1)}, u32[]{:S(2)}) copy-start(bf16[128,4096]{1,0:T(8,128)(2,1)} %param.6) | copy-start | bytes 3145732
  7.2 45.1 %all-gather.5.cloned.1.call-start = ((), (), s32[]{:S(2)}) async-start(), calls=%async_computation.6 | async-start | bytes 1179648 | tf_op jit(solution)/shard_map/all_gather | solution.py:40
  7.9 84.9 %all-gather.9.cloned.1.call-start = ((), (), s32[]{:S(2)}) async-start(), calls=%async_computation.8 | async-start | bytes 1179648 | tf_op jit(solution)/shard_map/all_gather | solution.py:37
  8.7 136.0 %all-gather.11.cloned.1.call-start = ((), (), s32[]{:S(2)}) async-start(), calls=%async_computation.9 | async-start | bytes 2359296 | tf_op jit(solution)/shard_map/all_gather | solution.py:38
  9.4 186.5 %all-gather.7.cloned.1.call-start = ((), (), s32[]{:S(2)}) async-start(), calls=%async_computation.7 | async-start | bytes 2359296 | tf_op jit(solution)/shard_map/all_gather | solution.py:39
  56.4 40.2 %all-to-all-start = ((bf16[128,128,32]{0,2,1:T(8,128)(2,1)}), bf16[128,128,32]{0,2,1:T(8,128)(2,1)S(1)}, u32[]{:S(2)}, u32[]{:S(2)}) async-start(bf16[128,128,32]{0,2,1:T(8,128)(2,1)} %copy.68), calls=%async_computation | async-start | bytes 2097152 | tf_op jit(solution)/shard_map/all_to_all | solution.py:28
  96.6 18.0 %all-to-all-start.1 = ((bf16[128,32,128]{0,1,2:T(8,128)(2,1)}), bf16[128,32,128]{0,1,2:T(8,128)(2,1)S(1)}, u32[]{:S(2)}, u32[]{:S(2)}) async-start(bf16[128,32,128]{0,1,2:T(8,128)(2,1)} %copy.72), calls=%async_computation.1 | async-start | bytes 2097152 | tf_op jit(solution)/shard_map/all_to_all | solution.py:21
  201.2 7.0 %copy-start.6 = (bf16[128,32,4,32]{0,3,2,1:T(8,128)(2,1)S(1)}, bf16[128,32,4,32]{0,3,2,1:T(8,128)(2,1)}, u32[]{:S(2)}) copy-start(bf16[128,32,4,32]{0,3,2,1:T(8,128)(2,1)} %copy.69) | copy-start | bytes 3145732
  203.9 18.8 %all-to-all-start.3 = ((bf16[128,32,128]{0,1,2:T(8,128)(2,1)}), bf16[128,32,128]{0,1,2:T(8,128)(2,1)}, u32[]{:S(2)}, u32[]{:S(2)}) async-start(bf16[128,32,128]{0,1,2:T(8,128)(2,1)} %copy.83), calls=%async_computation.5 | async-start | bytes 2097152 | tf_op jit(solution)/shard_map/all_to_all | solution.py:21
  208.2 7.5 %copy-start.1 = (bf16[32,128,256]{2,1,0:T(8,128)(2,1)S(1)}, bf16[32,128,256]{2,1,0:T(8,128)(2,1)}, u32[]{:S(2)}) copy-start(bf16[32,128,256]{2,1,0:T(8,128)(2,1)} %all-gather.11.cloned.1.call-done) | copy-start | bytes 6291460
  214.4 1.3 copy-start.2
  222.7 18.0 %all-to-all-start.2 = ((bf16[128,128,32]{0,2,1:T(8,128)(2,1)}), bf16[128,128,32]{0,2,1:T(8,128)(2,1)S(1)}, u32[]{:S(2)}, u32[]{:S(2)}) async-start(bf16[128,128,32]{0,2,1:T(8,128)(2,1)} %copy.76), calls=%async_computation.2 | async-start | bytes 2097152 | tf_op jit(solution)/shard_map/all_to_all | solution.py:28
  226.3 176.2 %all-reduce.3.cloned.1.call-start = ((), (), s32[]{:S(2)}) async-start(), calls=%async_computation.12 | async-start | bytes 8388608 | tf_op jit(solution)/shard_map/psum | solution.py:71
  240.7 1.0 copy-start.4
  241.7 3.2 copy-start.5
  248.3 244.9 %reduce-scatter.5.cloned.1.call-start = ((), (), s32[]{:S(2)}) async-start(), calls=%async_computation.11 | async-start | bytes 4718592 | tf_op jit(solution)/shard_map/reduce_scatter | solution.py:69
  254.5 331.1 %reduce-scatter.3.cloned.1.call-start = ((), (), s32[]{:S(2)}) async-start(), calls=%async_computation.10 | async-start | bytes 4718592 | tf_op jit(solution)/shard_map/reduce_scatter | solution.py:68
  258.9 1.2 copy-start.3
Sparse Core Ops, SparseCore 0:
  10.1 42.2 all-gather.4
  54.4 38.4 all-gather.8
  94.9 49.7 all-gather.10
  146.6 49.2 all-gather.6
  248.4 153.9 all-reduce.2
  405.9 87.2 reduce-scatter.4
  497.3 88.2 reduce-scatter.2
where the time goes:
time: 595 us; the launch traced here: 594 us
  waiting for transfers between devices  495 us (83%)
  matrix products  38.1 us (6%)
  local copies, waits for them, and re-layouts  23.5 us (4%)
  starting transfers between devices  15.3 us (3%)
  between operations  14.2 us (2%)
  other arithmetic  7.74 us (1%)
    psum x1, waiting for transfers between devices, per_device(): square_sum = lax.psum((grad_uf, grad_ds), 'dp')  139 us
    reduce_scatter x1, waiting for transfers between devices, per_device(): lax.psum_scatter(grad_us, 'dp', scatter_dimension=1, tiled=True)  90.4 us
    reduce_scatter x1, waiting for transfers between devices, per_device(): lax.psum_scatter(grad_df, 'dp', scatter_dimension=1, tiled=True)  82.1 us
    all_gather x1, waiting for transfers between devices, per_device(): lax.all_gather(down_first, 'dp', axis=1, tiled=True)  46.8 us
    all_gather x1, waiting for transfers between devices, per_device(): lax.all_gather(down_second, 'dp', axis=1, tiled=True)  42.4 us
    all_gather x1, waiting for transfers between devices, per_device(): lax.all_gather(up_first, 'dp', axis=1, tiled=True)  32.9 us
    all_gather x1, waiting for transfers between devices, per_device(): lax.all_gather(up_second, 'dp', axis=1, tiled=True)  29.7 us
    all_to_all x2, waiting for transfers between devices, permute_forward(): lax.all_to_all(lower, 'blk', split_axis=2, concat_axis=1, tiled=True)  17.9 us
  transfers between devices with their start and end apart: 11, of which 10 were waited for; matrix products, arithmetic and copies ran while one was open for 8% of the time, Pallas kernels for 0%

commit v1 on v0

--- a/solution.py
+++ b/solution.py
@@ -1,9 +1,397 @@
+import functools
 import math
 
 import jax
 import jax.numpy as jnp
 from jax import lax
+from jax.experimental import pallas as pl
+from jax.experimental.pallas import tpu as pltpu
 from jax.sharding import PartitionSpec as P
+
+SIDE = 2
+VMEM_BYTES = 50 * 1024 * 1024
+
+
+class Place:
+    def __init__(self, size):
+        self.depth = size // SIDE
+        me = lax.axis_index("dp")
+        self.z = lax.div(me, SIDE)
+        self.x = lax.rem(me, SIDE)
+        self.me = me
+        self.partner = self.z * SIDE + (1 - self.x)
+
+    def chunk(self, z, x):
+        return z * SIDE + x
+
+    def has_below(self):
+        return self.z > 0
+
+    def has_above(self):
+        return self.z < self.depth - 1
+
+
+def greet(place):
+    barrier = pltpu.get_barrier_semaphore()
+
+    def tell(target):
+        pl.semaphore_signal(
+            barrier, inc=1, device_id={"dp": target}, device_id_type=pl.DeviceIdType.MESH
+        )
+
+    tell(place.partner)
+    pl.when(place.has_below())(lambda: tell(place.me - SIDE))
+    pl.when(place.has_above())(lambda: tell(place.me + SIDE))
+    inner = jnp.logical_and(place.has_below(), place.has_above())
+    pl.when(inner)(lambda: pl.semaphore_wait(barrier, 3))
+    pl.when(jnp.logical_not(inner))(lambda: pl.semaphore_wait(barrier, 2))
+
+
+def rows_of(ref, index, rows):
+    return ref.at[:, pl.ds(pl.multiple_of(index * rows, rows), rows), :]
+
+
+def send(src, dst, send_sem, recv_sem, target):
+    return pltpu.make_async_remote_copy(
+        src_ref=src,
+        dst_ref=dst,
+        send_sem=send_sem,
+        recv_sem=recv_sem,
+        device_id={"dp": target},
+        device_id_type=pl.DeviceIdType.MESH,
+    )
+
+
+class Gather:
+    def __init__(self, place, own, out, rows, local_sem, sends, recv, wide):
+        self.p, self.own, self.out, self.rows, self.wide = place, own, out, rows, wide
+        self.local_sem, self.sends, self.recv = local_sem, sends, recv
+
+    def _copy(self, index, way, target):
+        mine = rows_of(self.out, index, self.rows)
+        return send(mine, mine, self.sends.at[way, index], self.recv.at[index], target)
+
+    def _own(self, way, target):
+        me = self.p.me
+        return send(
+            self.own,
+            rows_of(self.out, me, self.rows),
+            self.sends.at[way, me],
+            self.recv.at[me],
+            target,
+        )
+
+    def _local(self):
+        return pltpu.make_async_copy(
+            self.own, rows_of(self.out, self.p.me, self.rows), self.local_sem
+        )
+
+    def across(self, index):
+        return self._copy(index, 0, self.p.partner)
+
+    def up(self, index):
+        return self._copy(index, 1, self.p.me + SIDE)
+
+    def down(self, index):
+        return self._copy(index, 2, self.p.me - SIDE)
+
+    def begin(self):
+        p = self.p
+        pl.when(p.has_above())(lambda: self._own(1, p.me + SIDE).start())
+        pl.when(p.has_below())(lambda: self._own(2, p.me - SIDE).start())
+        self._own(0, p.partner).start()
+        self._local().start()
+
+    def landed(self, index):
+        self._copy(index, 0, self.p.partner).wait_recv()
+
+    def begin_wide(self):
+        p = self.p
+        if self.wide:
+            self.landed(p.partner)
+            pl.when(p.has_above())(lambda: self.up(p.partner).start())
+            pl.when(p.has_below())(lambda: self.down(p.partner).start())
+
+    def step(self, distance):
+        p = self.p
+        columns = (p.x, 1 - p.x) if self.wide else (p.x,)
+        for x in columns:
+
+            def from_below():
+                index = p.chunk(p.z - distance, x)
+                self.landed(index)
+                pl.when(p.has_above())(lambda: self.up(index).start())
+                if not self.wide:
+                    self.across(index).start()
+
+            def from_above():
+                index = p.chunk(p.z + distance, x)
+                self.landed(index)
+                pl.when(p.has_below())(lambda: self.down(index).start())
+                if not self.wide:
+                    self.across(index).start()
+
+            pl.when(p.z >= distance)(from_below)
+            pl.when(p.z + distance < p.depth)(from_above)
+
+    def finish(self):
+        p = self.p
+        if not self.wide:
+            for z in range(p.depth):
+                self.landed(p.chunk(z, 1 - p.x))
+        self._local().wait()
+        self._own(0, p.partner).wait_send()
+        columns = (p.x, 1 - p.x) if self.wide else (p.x,)
+        for x in columns:
+            here = p.chunk(p.z, x)
+            pl.when(p.has_above())(lambda: self.up(here).wait_send())
+            pl.when(p.has_below())(lambda: self.down(here).wait_send())
+            for distance in range(1, p.depth):
+
+                def below():
+                    index = p.chunk(p.z - distance, x)
+                    pl.when(p.has_above())(lambda: self.up(index).wait_send())
+                    if not self.wide:
+                        self.across(index).wait_send()
+
+                def above():
+                    index = p.chunk(p.z + distance, x)
+                    pl.when(p.has_below())(lambda: self.down(index).wait_send())
+                    if not self.wide:
+                        self.across(index).wait_send()
+
+                pl.when(p.z >= distance)(below)
+                pl.when(p.z + distance < p.depth)(above)
+
+
+def run_gathers(gathers, depth):
+    for gather in gathers:
+        gather.begin()
+    for gather in gathers:
+        gather.begin_wide()
+    for distance in range(1, depth):
+        for gather in gathers:
+            gather.step(distance)
+    for gather in gathers:
+        gather.finish()
+
+
+def gather_kernel(size, count, *refs):
+    owns, outs = refs[:count], refs[count : 2 * count]
+    local, sends, recv = refs[2 * count :]
+    place = Place(size)
+    greet(place)
+    gathers = [
+        Gather(
+            place, owns[a], outs[a], owns[a].shape[1],
+            local.at[a], sends.at[a], recv.at[a], a == 0,
+        )
+        for a in range(count)
+    ]
+    run_gathers(gathers, place.depth)
+
+
+def gather_rows(arrays, size):
+    count = len(arrays)
+    anywhere = pl.BlockSpec(memory_space=pl.ANY)
+    return pl.pallas_call(
+        functools.partial(gather_kernel, size, count),
+        out_shape=tuple(
+            jax.ShapeDtypeStruct((a.shape[0], a.shape[1] * size, a.shape[2]), a.dtype)
+            for a in arrays
+        ),
+        in_specs=[anywhere] * count,
+        out_specs=tuple([anywhere] * count),
+        scratch_shapes=[
+            pltpu.SemaphoreType.DMA((count,)),
+            pltpu.SemaphoreType.DMA((count, 3, size)),
+            pltpu.SemaphoreType.DMA((count, size)),
+        ],
+        compiler_params=pltpu.CompilerParams(collective_id=0, has_side_effects=True),
+        name="gather_rows",
+    )(*arrays)
+
+
+class Reduce:
+    def __init__(self, place, grad, rows, scale, final, cross, low, high, stage, sems):
+        self.p, self.grad, self.rows, self.scale, self.final = place, grad, rows, scale, final
+        self.cross, self.low, self.high, self.stage, self.sems = cross, low, high, stage, sems
+
+    def _cross(self, z):
+        p = self.p
+        return send(
+            rows_of(self.grad, p.chunk(z, 1 - p.x), self.rows),
+            self.cross.at[z],
+            self.sems.at[0, z],
+            self.sems.at[1, z],
+            p.partner,
+        )
+
+    def _up(self, z):
+        return send(
+            self.stage.at[z], self.low.at[z], self.sems.at[2, z], self.sems.at[3, z],
+            self.p.me + SIDE,
+        )
+
+    def _down(self, z):
+        return send(
+            self.stage.at[z], self.high.at[z], self.sems.at[4, z], self.sems.at[5, z],
+            self.p.me - SIDE,
+        )
+
+    def send_across(self, distance):
+        p = self.p
+        if distance == 0:
+            self._cross(p.z).start()
+            return
+        pl.when(p.z + distance < p.depth)(lambda: self._cross(p.z + distance).start())
+        pl.when(p.z >= distance)(lambda: self._cross(p.z - distance).start())
+
+    def _sum(self, z, others, store):
+        first = pl.multiple_of(self.p.chunk(z, self.p.x) * self.rows, self.rows)
+
+        @pl.loop(0, self.grad.shape[0], unroll=2)
+        def _(block):
+            total = self.grad[block, pl.ds(first, self.rows), :].astype(jnp.float32)
+            for other in (self.cross,) + others:
+                total = total + other[z, block].astype(jnp.float32)
+            store(block, total)
+
+    def step(self, distance):
+        p = self.p
+
+        def upward():
+            z = p.z + distance
+            self._cross(z).wait_recv()
+
+            def store(block, total):
+                self.stage[z, block] = total.astype(self.stage.dtype)
+
+            def joined():
+                self._up(z).wait_recv()
+                self._sum(z, (self.low,), store)
+
+            pl.when(p.has_below())(joined)
+            pl.when(jnp.logical_not(p.has_below()))(lambda: self._sum(z, (), store))
+            self._up(z).start()
+
+        def downward():
+            z = p.z - distance
+            self._cross(z).wait_recv()
+
+            def store(block, total):
+                self.stage[z, block] = total.astype(self.stage.dtype)
+
+            def joined():
+                self._down(z).wait_recv()
+                self._sum(z, (self.high,), store)
+
+            pl.when(p.has_above())(joined)
+            pl.when(jnp.logical_not(p.has_above()))(lambda: self._sum(z, (), store))
+            self._down(z).start()
+
+        pl.when(p.z + distance < p.depth)(upward)
+        pl.when(p.z >= distance)(downward)
+
+    def last(self):
+        p = self.p
+
+        def store(block, total):
+            self.final[block] = (total * self.scale).astype(self.final.dtype)
+
+        self._cross(p.z).wait_recv()
+        pl.when(p.has_below())(lambda: self._up(p.z).wait_recv())
+        pl.when(p.has_above())(lambda: self._down(p.z).wait_recv())
+        low, high = p.has_below(), p.has_above()
+        pl.when(jnp.logical_and(low, high))(
+            lambda: self._sum(p.z, (self.low, self.high), store)
+        )
+        pl.when(jnp.logical_not(high))(lambda: self._sum(p.z, (self.low,), store))
+        pl.when(jnp.logical_not(low))(lambda: self._sum(p.z, (self.high,), store))
+
+    def finish(self):
+        p = self.p
+        for z in range(p.depth):
+            self._cross(z).wait_send()
+        for distance in range(1, p.depth):
+            pl.when(p.z + distance < p.depth)(lambda: self._up(p.z + distance).wait_send())
+            pl.when(p.z >= distance)(lambda: self._down(p.z - distance).wait_send())
+
+
+def reduce_kernel(size, scale, shared, *refs):
+    count = 4
+    grads, outs = refs[:count], refs[count : 2 * count]
+    rest = refs[2 * count :]
+    crosses, lows, highs, stages = (rest[k * count : (k + 1) * count] for k in range(4))
+    finals = rest[4 * count : 4 * count + shared]
+    sems, local, sends, recv = rest[4 * count + shared :]
+    place = Place(size)
+    greet(place)
+    reduces = [
+        Reduce(
+            place, grads[a], grads[a].shape[1] // size, scale,
+            finals[a] if a < shared else outs[a],
+            crosses[a], lows[a], highs[a], stages[a], sems.at[a],
+        )
+        for a in range(count)
+    ]
+    gathers = [
+        Gather(
+            place, finals[a], outs[a], finals[a].shape[1],
+            local.at[a], sends.at[a], recv.at[a], False,
+        )
+        for a in range(shared)
+    ]
+    for distance in range(place.depth - 1, -1, -1):
+        for reduce in reduces:
+            reduce.send_across(distance)
+    for distance in range(place.depth - 1, 0, -1):
+        for reduce in reduces:
+            reduce.step(distance)
+    for a in range(shared):
+        reduces[a].last()
+        gathers[a].begin()
+    for a in range(shared, count):
+        reduces[a].last()
+    for distance in range(1, place.depth):
+        for gather in gathers:
+            gather.step(distance)
+    for gather in gathers:
+        gather.finish()
+    for reduce in reduces:
+        reduce.finish()
+
+
+def reduce_rows(grads, shared, size, scale):
+    depth = size // SIDE
+    parts = [(g.shape[0], g.shape[1] // size, g.shape[2]) for g in grads]
+    slots = [pltpu.VMEM((depth,) + part, jnp.bfloat16) for part in parts]
+    vmem = pl.BlockSpec(memory_space=pltpu.VMEM)
+    anywhere = pl.BlockSpec(memory_space=pl.ANY)
+    count = len(grads)
+    return pl.pallas_call(
+        functools.partial(reduce_kernel, size, scale, shared),
+        out_shape=tuple(
+            jax.ShapeDtypeStruct(g.shape, jnp.bfloat16)
+            if a < shared
+            else jax.ShapeDtypeStruct(parts[a], jnp.float32)
+            for a, g in enumerate(grads)
+        ),
+        in_specs=[vmem] * count,
+        out_specs=tuple(anywhere if a < shared else vmem for a in range(count)),
+        scratch_shapes=slots * 4
+        + [pltpu.VMEM(parts[a], jnp.bfloat16) for a in range(shared)]
+        + [
+            pltpu.SemaphoreType.DMA((count, 6, depth)),
+            pltpu.SemaphoreType.DMA((shared,)),
+            pltpu.SemaphoreType.DMA((shared, 3, size)),
+            pltpu.SemaphoreType.DMA((shared, size)),
+        ],
+        compiler_params=pltpu.CompilerParams(
+            collective_id=1, has_side_effects=True, vmem_limit_bytes=VMEM_BYTES
+        ),
+        name="reduce_rows",
+    )(*grads)
 
 
 def activation(values):
@@ -33,13 +421,15 @@
     local_blocks = up_first.shape[0]
     block_size = up_first.shape[2]
     factor = 1.0 / math.sqrt(tok_rows * lax.axis_size("dp"))
-    gathered = (
-        lax.all_gather(up_first, "dp", axis=1, tiled=True),
-        lax.all_gather(up_second, "dp", axis=1, tiled=True),
-        lax.all_gather(down_first, "dp", axis=1, tiled=True),
-        lax.all_gather(down_second, "dp", axis=1, tiled=True),
-    )
-    full_uf, full_us, full_df, full_ds = gathered
+    size = lax.axis_size("dp")
+    weights = (down_second, up_first, up_second, down_first)
+    tiled = size % SIDE == 0 and size > SIDE and all(w.shape[1] % 16 == 0 for w in weights)
+    if tiled:
+        full_ds, full_uf, full_us, full_df = gather_rows(weights, size)
+    else:
+        full_ds, full_uf, full_us, full_df = (
+            lax.all_gather(w, "dp", axis=1, tiled=True) for w in weights
+        )
     inputs_b = tokens.reshape(tok_rows, local_blocks, block_size)
     first_up = jnp.einsum(
         "tbi,bij->tbj", inputs_b, full_uf, preferred_element_type=jnp.float32
@@ -64,6 +454,14 @@
         "tbj,bij->tbi", back_up, full_uf, preferred_element_type=jnp.float32
     ).astype(jnp.bfloat16)
     input_grad = input_grad.reshape(tok_rows, local_blocks * block_size)
+    if tiled:
+        grads = (grad_ds, grad_uf, grad_us, grad_df)
+        grad_ds, grad_uf, grad_us, grad_df = reduce_rows(
+            tuple(g.astype(jnp.bfloat16) for g in grads), 2, size, factor
+        )
+        grad_ds = grad_ds.astype(jnp.float32)
+        grad_uf = grad_uf.astype(jnp.float32)
+        return (input_grad, grad_uf, grad_us, grad_df, grad_ds)
     wide_sum = (
         lax.psum_scatter(grad_us, "dp", scatter_dimension=1, tiled=True),
         lax.psum_scatter(grad_df, "dp", scatter_dimension=1, tiled=True),

time: 595 us -> 269 us (0.45)
  waiting for transfers between devices: 495 us -> 36.4 us
  Pallas kernels: 0 us -> 170 us
  between operations: 14.2 us -> 0.88 us
  matrix products: 38.1 us -> 26 us
  local copies, waits for them, and re-layouts: 23.5 us -> 15.6 us
    reduce_scatter x2 -> x0, waiting for transfers between devices: 173 us -> none  [the longest x1 90.4 us: per_device(): lax.psum_scatter(grad_us, 'dp', scatter_dimension=1, tiled=True)]
    pallas_call x0 -> x2, Pallas kernels: none -> 170 us  [the longest x1 96.5 us: reduce_rows(): pl.pallas_call(functools.partial(reduce_kernel, size, scale, shared), out...]
    all_gather x4 -> x0, waiting for transfers between devices: 152 us -> none  [the longest x1 46.8 us: per_device(): lax.all_gather(down_first, 'dp', axis=1, tiled=True)]
    psum x1 -> x0, waiting for transfers between devices: 139 us -> none  [per_device(): square_sum = lax.psum((grad_uf, grad_ds), 'dp')]
    mul x3 -> x0, other arithmetic: 7.74 us -> none  [the longest x1 3.99 us: per_device(): grad_ds = square_sum[1] * factor]
    unnamed x17 -> x25, local copies, waits for them, and re-layouts: 10.5 us -> 3.55 us
  transfers between devices with their start and end apart: 11 -> 4, of which waited for: 10 -> 4; matrix products, arithmetic and copies ran while one was open for 8% -> 8% of each run, Pallas kernels for 0% -> 0%
where the time goes in v1:
time: 269 us; the launch traced here: 268 us
  Pallas kernels  170 us (63%)
  waiting for transfers between devices  36.4 us (14%)
  matrix products  26 us (10%)
  starting transfers between devices  16.5 us (6%)
  local copies, waits for them, and re-layouts  15.6 us (6%)
  other arithmetic  3.13 us (1%)
    pallas_call x1, Pallas kernels, reduce_rows(): pl.pallas_call(functools.partial(reduce_kernel, size, scale, shared), out...  96.5 us
    pallas_call x1, Pallas kernels, gather_rows(): pl.pallas_call(functools.partial(gather_kernel, size, count), out_shape=t...  73.6 us
    all_to_all x2, waiting for transfers between devices, permute_forward(): lax.all_to_all(lower, 'blk', split_axis=2, concat_axis=1, tiled=True)  19.6 us
    all_to_all x2, waiting for transfers between devices, permute_backward(): lax.all_to_all(spread, 'blk', split_axis=1, concat_axis=2, tiled=True)  16.8 us
    all_to_all x2, starting transfers between devices, permute_forward(): lax.all_to_all(lower, 'blk', split_axis=2, concat_axis=1, tiled=True)  8.5 us
    all_to_all x2, starting transfers between devices, permute_backward(): lax.all_to_all(spread, 'blk', split_axis=1, concat_axis=2, tiled=True)  7.96 us
  transfers between devices with their start and end apart: 4, of which 4 were waited for; matrix products, arithmetic and copies ran while one was open for 8% of the time, Pallas kernels for 0%

profile of v1, /device:TPU:0, one launch (start us, length us, event | category | flops | bytes accessed | tf_op | source)
XLA Modules:
  0.0 268.5 jit_solution(15941426842343471113)
XLA Ops:
  0.6 73.6 %gather_rows.1 = (bf16[32,128,128]{2,1,0:T(8,128)(2,1)}, bf16[32,128,128]{2,1,0:T(8,128)(2,1)}, bf16[32,128,256]{2,1,0:T(8,128)(2,1)}, bf16[32,256,128]{2,1,0:T(8,128)(2,1)}) custom-call(bf16[32,16,128]{2,1,0:T(8,128)(2,1)} %refs_0_.1, bf16[32,16,128]{2,1,0:T(8,128)(2,1)} %refs_1_.1, bf16[32,16,256]{2,1,0:T(8,128)(2,1)} %refs_2_.1, bf16[32,32,128]{2,1,0:T(8,128)(2,1)} %refs_3_.1), custom_call_target="tpu_custom_call" | custom-call | tf_op jit(solution)/shard_map/gather_rows/pallas_call | solution.py:197
  74.2 2.5 fusion.11
  76.7 1.7 copy.73
  78.4 3.5 %all-to-all-start = ((bf16[128,128,32]{0,2,1:T(8,128)(2,1)}), bf16[128,128,32]{0,2,1:T(8,128)(2,1)S(1)}, u32[]{:S(2)}, u32[]{:S(2)}) async-start(bf16[128,128,32]{0,2,1:T(8,128)(2,1)} %copy.73), calls=%async_computation | async-start | bytes 2097152 | tf_op jit(solution)/shard_map/all_to_all | solution.py:416
  82.8 1.7 copy.78
  84.4 11.9 %all-to-all-done = bf16[128,128,32]{0,2,1:T(8,128)(2,1)S(1)} async-done(((bf16[128,128,32]{0,2,1:T(8,128)(2,1)}), bf16[128,128,32]{0,2,1:T(8,128)(2,1)S(1)}, u32[]{:S(2)}, u32[]{:S(2)}) %all-to-all-start) | async-done | bytes 1048608 | tf_op jit(solution)/shard_map/all_to_all | solution.py:416
  96.3 4.2 %all-to-all-start.1 = ((bf16[128,32,128]{0,1,2:T(8,128)(2,1)}), bf16[128,32,128]{0,1,2:T(8,128)(2,1)}, u32[]{:S(2)}, u32[]{:S(2)}) async-start(bf16[128,32,128]{0,1,2:T(8,128)(2,1)} %copy.78), calls=%async_computation.1 | async-start | bytes 2097152 | tf_op jit(solution)/shard_map/all_to_all | solution.py:409
  101.7 13.4 %all-to-all-done.1 = bf16[128,32,128]{0,1,2:T(8,128)(2,1)} async-done(((bf16[128,32,128]{0,1,2:T(8,128)(2,1)}), bf16[128,32,128]{0,1,2:T(8,128)(2,1)}, u32[]{:S(2)}, u32[]{:S(2)}) %all-to-all-start.1) | async-done | bytes 1048608 | tf_op jit(solution)/shard_map/all_to_all | solution.py:409
  115.1 1.6 copy.80
  116.8 2.6 fusion.24
  119.4 3.2 %fusion.6 = bf16[128,32,256]{0,2,1:T(8,128)(2,1)S(1)} fusion(f32[32,256,128]{2,1,0:T(8,128)S(1)} %fusion.24, bf16[32,256,128]{2,1,0:T(8,128)(2,1)S(1)} %copy-done.10, bf16[128,32,128]{0,2,1:T(8,128)(2,1)S(1)} %bitcast.102), kind=kOutput, calls=%fused_computation.8 | convolution fusion | flops 289406976 | bytes 9437184 | tf_op jit(solution)/shard_map/tbj,bij->tbi/dot_general | solution.py:447
  124.0 1.6 copy.84
  125.6 4.4 %all-to-all-start.2 = ((bf16[128,128,32]{0,2,1:T(8,128)(2,1)}), bf16[128,128,32]{0,2,1:T(8,128)(2,1)}, u32[]{:S(2)}, u32[]{:S(2)}) async-start(bf16[128,128,32]{0,2,1:T(8,128)(2,1)} %copy.84), calls=%async_computation.2 | async-start | bytes 2097152 | tf_op jit(solution)/shard_map/all_to_all | solution.py:416
  130.1 4.9 %fusion.14 = bf16[128,32,128]{0,2,1:T(8,128)(2,1)S(1)} fusion(bf16[32,256,128]{2,1,0:T(8,128)(2,1)} %get-tuple-element.15, f32[32,256,128]{2,1,0:T(8,128)} %copy-done.5), kind=kOutput, calls=%fused_computation.28 | convolution fusion | flops 278396928 | bytes 7340032 | tf_op jit(solution)/shard_map/tbi,bij->tbj/dot_general | solution.py:439
  135.0 1.7 copy.89
  136.6 2.9 %convolution_convert_fusion.refs_3_ = bf16[32,256,128]{2,1,0:T(8,128)(2,1)} fusion(bf16[128,32,128]{0,2,1:T(8,128)(2,1)S(1)} %bitcast.103, f32[32,256,128]{2,1,0:T(8,128)S(1)} %copy-done.6), kind=kOutput, calls=%fused_computation.16 | convolution fusion | flops 278921216 | bytes 7340032 | tf_op jit(solution)/shard_map/tbi,tbj->bij/dot_general | solution.py:446
  139.5 4.9 %all-to-all-done.2 = bf16[128,128,32]{0,2,1:T(8,128)(2,1)} async-done(((bf16[128,128,32]{0,2,1:T(8,128)(2,1)}), bf16[128,128,32]{0,2,1:T(8,128)(2,1)}, u32[]{:S(2)}, u32[]{:S(2)}) %all-to-all-start.2) | async-done | bytes 1048608 | tf_op jit(solution)/shard_map/all_to_all | solution.py:416
  144.4 4.2 %all-to-all-start.3 = ((bf16[128,32,128]{0,1,2:T(8,128)(2,1)}), bf16[128,32,128]{0,1,2:T(8,128)(2,1)}, u32[]{:S(2)}, u32[]{:S(2)}) async-start(bf16[128,32,128]{0,1,2:T(8,128)(2,1)} %copy.89), calls=%async_computation.3 | async-start | bytes 2097152 | tf_op jit(solution)/shard_map/all_to_all | solution.py:409
  148.7 3.6 %convolution_convert_fusion.1.refs_2_ = bf16[32,128,256]{2,1,0:T(8,128)(2,1)} fusion(bf16[128,32,256]{0,2,1:T(8,128)(2,1)} %copy-done.2, bf16[128,128,32]{0,2,1:T(8,128)(2,1)S(1)} %bitcast.96), kind=kOutput, calls=%fused_computation.17 | convolution fusion | flops 269484032 | bytes 5242880 | tf_op jit(solution)/shard_map/tbj,tjk->jbk/dot_general | solution.py:450
  155.1 1.9 fusion.15.refs_1_
  157.0 6.2 %all-to-all-done.3 = bf16[128,32,128]{0,1,2:T(8,128)(2,1)} async-done(((bf16[128,32,128]{0,1,2:T(8,128)(2,1)}), bf16[128,32,128]{0,1,2:T(8,128)(2,1)}, u32[]{:S(2)}, u32[]{:S(2)}) %all-to-all-start.3) | async-done | bytes 1048608 | tf_op jit(solution)/shard_map/all_to_all | solution.py:409
  167.3 96.5 %reduce_rows.1 = (bf16[32,128,128]{2,1,0:T(8,128)(2,1)S(1)}, bf16[32,128,128]{2,1,0:T(8,128)(2,1)S(1)}, f32[32,16,256]{2,1,0:T(8,128)S(1)}, f32[32,32,128]{2,1,0:T(8,128)S(1)}) custom-call(bf16[32,128,128]{2,1,0:T(8,128)(2,1)} %convolution_convert_fusion.3.refs_0_, bf16[32,128,128]{2,1,0:T(8,128)(2,1)} %fusion.15.refs_1_, ...), custom_call_target="tpu_custom_call" | custom-call | tf_op jit(solution)/shard_map/reduce_rows/pallas_call | solution.py:372
  263.8 1.6 convert_element_type.73
  265.3 1.6 convert_element_type.74
  (32 shorter events, 11.8 us)
Async XLA Ops:
  0.6 81.3 %copy-start = (bf16[128,4096]{1,0:T(8,128)(2,1)S(1)}, bf16[128,4096]{1,0:T(8,128)(2,1)}, u32[]{:S(2)}) copy-start(bf16[128,4096]{1,0:T(8,128)(2,1)} %param.6) | copy-start | bytes 3145732
  74.2 7.7 %copy-start.4 = (bf16[32,128,128]{2,1,0:T(8,128)(2,1)S(1)}, bf16[32,128,128]{2,1,0:T(8,128)(2,1)}, u32[]{:S(2)}) copy-start(bf16[32,128,128]{2,1,0:T(8,128)(2,1)} %get-tuple-element.13) | copy-start | bytes 3145732
  78.4 18.0 %all-to-all-start = ((bf16[128,128,32]{0,2,1:T(8,128)(2,1)}), bf16[128,128,32]{0,2,1:T(8,128)(2,1)S(1)}, u32[]{:S(2)}, u32[]{:S(2)}) async-start(bf16[128,128,32]{0,2,1:T(8,128)(2,1)} %copy.73), calls=%async_computation | async-start | bytes 2097152 | tf_op jit(solution)/shard_map/all_to_all | solution.py:416
  96.3 18.8 %all-to-all-start.1 = ((bf16[128,32,128]{0,1,2:T(8,128)(2,1)}), bf16[128,32,128]{0,1,2:T(8,128)(2,1)}, u32[]{:S(2)}, u32[]{:S(2)}) async-start(bf16[128,32,128]{0,1,2:T(8,128)(2,1)} %copy.78), calls=%async_computation.1 | async-start | bytes 2097152 | tf_op jit(solution)/shard_map/all_to_all | solution.py:409
  116.7 2.6 copy-start.8
  116.7 2.6 copy-start.10
  119.4 3.3 %copy-start.5 = (f32[32,256,128]{2,1,0:T(8,128)}, f32[32,256,128]{2,1,0:T(8,128)S(1)}, u32[]{:S(2)}) copy-start(f32[32,256,128]{2,1,0:T(8,128)S(1)} %fusion.24) | copy-start | bytes 12582916
  119.4 3.3 %copy-start.1 = (bf16[32,128,256]{2,1,0:T(8,128)(2,1)S(1)}, bf16[32,128,256]{2,1,0:T(8,128)(2,1)}, u32[]{:S(2)}) copy-start(bf16[32,128,256]{2,1,0:T(8,128)(2,1)} %get-tuple-element.14) | copy-start | bytes 6291460
  122.6 1.3 copy-start.2
  125.6 18.8 %all-to-all-start.2 = ((bf16[128,128,32]{0,2,1:T(8,128)(2,1)}), bf16[128,128,32]{0,2,1:T(8,128)(2,1)}, u32[]{:S(2)}, u32[]{:S(2)}) async-start(bf16[128,128,32]{0,2,1:T(8,128)(2,1)} %copy.84), calls=%async_computation.2 | async-start | bytes 2097152 | tf_op jit(solution)/shard_map/all_to_all | solution.py:416
  130.1 6.6 %copy-start.6 = (f32[32,256,128]{2,1,0:T(8,128)S(1)}, f32[32,256,128]{2,1,0:T(8,128)}, u32[]{:S(2)}) copy-start(f32[32,256,128]{2,1,0:T(8,128)} %copy-done.5) | copy-start | bytes 12582916
  130.1 6.6 %copy-start.9 = (bf16[128,32,4,32]{0,3,2,1:T(8,128)(2,1)S(1)}, bf16[128,32,4,32]{0,3,2,1:T(8,128)(2,1)}, u32[]{:S(2)}) copy-start(bf16[128,32,4,32]{0,3,2,1:T(8,128)(2,1)} %copy.74) | copy-start | bytes 3145732
  144.4 18.8 %all-to-all-start.3 = ((bf16[128,32,128]{0,1,2:T(8,128)(2,1)}), bf16[128,32,128]{0,1,2:T(8,128)(2,1)}, u32[]{:S(2)}, u32[]{:S(2)}) async-start(bf16[128,32,128]{0,1,2:T(8,128)(2,1)} %copy.89), calls=%async_computation.3 | async-start | bytes 2097152 | tf_op jit(solution)/shard_map/all_to_all | solution.py:409
  153.7 10.9 %copy-start.3 = (bf16[128,4096]{1,0:T(8,128)(2,1)S(1)}, bf16[128,4096]{1,0:T(8,128)(2,1)}, u32[]{:S(2)}) copy-start(bf16[128,4096]{1,0:T(8,128)(2,1)} %param.11) | copy-start | bytes 3145732
  155.1 10.9 %copy-start.7 = (bf16[32,128,128]{2,1,0:T(8,128)(2,1)S(1)}, bf16[32,128,128]{2,1,0:T(8,128)(2,1)}, u32[]{:S(2)}) copy-start(bf16[32,128,128]{2,1,0:T(8,128)(2,1)} %convolution_convert_fusion.5) | copy-start | bytes 3145732

commit v2 on v1

--- a/solution.py
+++ b/solution.py
@@ -42,9 +42,17 @@
     tell(place.partner)
     pl.when(place.has_below())(lambda: tell(place.me - SIDE))
     pl.when(place.has_above())(lambda: tell(place.me + SIDE))
+    spread = lax.axis_size("blk")
+    for hop in range(1, spread):
+        pl.semaphore_signal(
+            barrier,
+            inc=1,
+            device_id={"blk": lax.rem(lax.axis_index("blk") + hop, spread)},
+            device_id_type=pl.DeviceIdType.MESH,
+        )
     inner = jnp.logical_and(place.has_below(), place.has_above())
-    pl.when(inner)(lambda: pl.semaphore_wait(barrier, 3))
-    pl.when(jnp.logical_not(inner))(lambda: pl.semaphore_wait(barrier, 2))
+    pl.when(inner)(lambda: pl.semaphore_wait(barrier, spread + 2))
+    pl.when(jnp.logical_not(inner))(lambda: pl.semaphore_wait(barrier, spread + 1))
 
 
 def rows_of(ref, index, rows):
@@ -164,21 +172,48 @@
                 pl.when(p.z + distance < p.depth)(above)
 
 
-def run_gathers(gathers, depth):
-    for gather in gathers:
-        gather.begin()
-    for gather in gathers:
-        gather.begin_wide()
-    for distance in range(1, depth):
-        for gather in gathers:
-            gather.step(distance)
-    for gather in gathers:
-        gather.finish()
-
-
-def gather_kernel(size, count, *refs):
-    owns, outs = refs[:count], refs[count : 2 * count]
-    local, sends, recv = refs[2 * count :]
+class Exchange:
+    def __init__(self, made, out, local_sem, sends, recv):
+        self.made, self.out, self.local_sem, self.sends, self.recv = made, out, local_sem, sends, recv
+        self.count = lax.axis_size("blk")
+        self.blocks = made.shape[0]
+        self.part = made.shape[1] // self.count
+        self.me = lax.axis_index("blk")
+
+    def _copy(self, hop):
+        target = lax.rem(self.me + hop, self.count)
+        return pltpu.make_async_remote_copy(
+            src_ref=rows_of(self.made, target, self.part),
+            dst_ref=self.out.at[pl.ds(self.me * self.blocks, self.blocks)],
+            send_sem=self.sends.at[hop],
+            recv_sem=self.recv.at[hop],
+            device_id={"blk": target},
+            device_id_type=pl.DeviceIdType.MESH,
+        )
+
+    def _local(self):
+        return pltpu.make_async_copy(
+            rows_of(self.made, self.me, self.part),
+            self.out.at[pl.ds(self.me * self.blocks, self.blocks)],
+            self.local_sem,
+        )
+
+    def begin(self):
+        for hop in range(1, self.count):
+            self._copy(hop).start()
+        self._local().start()
+
+    def finish(self):
+        for hop in range(1, self.count):
+            self._copy(hop).wait()
+        self._local().wait()
+
+
+def gather_kernel(size, *refs):
+    count = 4
+    owns, tokens, upstream = refs[:count], refs[count], refs[count + 1]
+    outs, moved_down, moved_up = refs[6 : 6 + count], refs[6 + count], refs[7 + count]
+    local, sends, recv, back, first, local_blk, sends_blk, recv_blk = refs[8 + count :]
     place = Place(size)
     greet(place)
     gathers = [
@@ -188,28 +223,79 @@
         )
         for a in range(count)
     ]
-    run_gathers(gathers, place.depth)
-
-
-def gather_rows(arrays, size):
+    down = Exchange(back, moved_down, local_blk.at[0], sends_blk.at[0], recv_blk.at[0])
+    up = Exchange(first, moved_up, local_blk.at[1], sends_blk.at[1], recv_blk.at[1])
+    blocks, width = first.shape[0], first.shape[1]
+    for gather in gathers:
+        gather.begin()
+    gathers[0].begin_wide()
+    for distance in range(1, place.depth):
+        for gather in gathers[:2]:
+            gather.step(distance)
+        if distance < place.depth - 1:
+            for gather in gathers[2:]:
+                gather.step(distance)
+    gathers[0].finish()
+
+    @pl.loop(0, blocks, unroll=2)
+    def _(block):
+        columns = pl.ds(pl.multiple_of(block * width, width), width)
+        back[block] = lax.dot_general(
+            outs[0][block], upstream[:, columns], (((1,), (1,)), ((), ())),
+            preferred_element_type=jnp.float32,
+        ).astype(jnp.bfloat16)
+
+    down.begin()
+    for gather in gathers[2:]:
+        gather.step(place.depth - 1)
+    gathers[1].finish()
+
+    @pl.loop(0, blocks, unroll=2)
+    def _(block):
+        columns = pl.ds(pl.multiple_of(block * width, width), width)
+        product = jnp.dot(
+            tokens[:, columns], outs[1][block], preferred_element_type=jnp.float32
+        )
+        first[block] = product.T.astype(jnp.bfloat16)
+
+    up.begin()
+    for gather in gathers[2:]:
+        gather.finish()
+    down.finish()
+    up.finish()
+
+
+def gather_rows(arrays, tokens, upstream, size):
     count = len(arrays)
+    vmem = pl.BlockSpec(memory_space=pltpu.VMEM)
     anywhere = pl.BlockSpec(memory_space=pl.ANY)
+    spread = lax.axis_size("blk")
+    blocks, width, rows = arrays[0].shape[0], arrays[0].shape[2], tokens.shape[0]
+    moved = jax.ShapeDtypeStruct((blocks * spread, width // spread, rows), jnp.bfloat16)
     return pl.pallas_call(
-        functools.partial(gather_kernel, size, count),
+        functools.partial(gather_kernel, size),
         out_shape=tuple(
             jax.ShapeDtypeStruct((a.shape[0], a.shape[1] * size, a.shape[2]), a.dtype)
             for a in arrays
-        ),
-        in_specs=[anywhere] * count,
-        out_specs=tuple([anywhere] * count),
+        )
+        + (moved, moved),
+        in_specs=[anywhere] * count + [vmem, vmem],
+        out_specs=(vmem, vmem) + (anywhere,) * (count - 2) + (anywhere, anywhere),
         scratch_shapes=[
             pltpu.SemaphoreType.DMA((count,)),
             pltpu.SemaphoreType.DMA((count, 3, size)),
             pltpu.SemaphoreType.DMA((count, size)),
+            pltpu.VMEM((blocks, width, rows), jnp.bfloat16),
+            pltpu.VMEM((blocks, width, rows), jnp.bfloat16),
+            pltpu.SemaphoreType.DMA((2,)),
+            pltpu.SemaphoreType.DMA((2, spread)),
+            pltpu.SemaphoreType.DMA((2, spread)),
         ],
-        compiler_params=pltpu.CompilerParams(collective_id=0, has_side_effects=True),
+        compiler_params=pltpu.CompilerParams(
+            collective_id=0, has_side_effects=True, vmem_limit_bytes=VMEM_BYTES
+        ),
         name="gather_rows",
-    )(*arrays)
+    )(*arrays, tokens, upstream)
 
 
 class Reduce:
@@ -416,20 +502,18 @@
     return lax.all_to_all(spread, "blk", split_axis=1, concat_axis=2, tiled=True)
 
 
-def per_device(tokens, up_first, up_second, down_first, down_second, cotangent):
+def by_collectives(tokens, up_first, up_second, down_first, down_second, cotangent):
     tok_rows = tokens.shape[0]
     local_blocks = up_first.shape[0]
     block_size = up_first.shape[2]
     factor = 1.0 / math.sqrt(tok_rows * lax.axis_size("dp"))
-    size = lax.axis_size("dp")
-    weights = (down_second, up_first, up_second, down_first)
-    tiled = size % SIDE == 0 and size > SIDE and all(w.shape[1] % 16 == 0 for w in weights)
-    if tiled:
-        full_ds, full_uf, full_us, full_df = gather_rows(weights, size)
-    else:
-        full_ds, full_uf, full_us, full_df = (
-            lax.all_gather(w, "dp", axis=1, tiled=True) for w in weights
-        )
+    gathered = (
+        lax.all_gather(up_first, "dp", axis=1, tiled=True),
+        lax.all_gather(up_second, "dp", axis=1, tiled=True),
+        lax.all_gather(down_first, "dp", axis=1, tiled=True),
+        lax.all_gather(down_second, "dp", axis=1, tiled=True),
+    )
+    full_uf, full_us, full_df, full_ds = gathered
     inputs_b = tokens.reshape(tok_rows, local_blocks, block_size)
     first_up = jnp.einsum(
         "tbi,bij->tbj", inputs_b, full_uf, preferred_element_type=jnp.float32
@@ -454,14 +538,6 @@
         "tbj,bij->tbi", back_up, full_uf, preferred_element_type=jnp.float32
     ).astype(jnp.bfloat16)
     input_grad = input_grad.reshape(tok_rows, local_blocks * block_size)
-    if tiled:
-        grads = (grad_ds, grad_uf, grad_us, grad_df)
-        grad_ds, grad_uf, grad_us, grad_df = reduce_rows(
-            tuple(g.astype(jnp.bfloat16) for g in grads), 2, size, factor
-        )
-        grad_ds = grad_ds.astype(jnp.float32)
-        grad_uf = grad_uf.astype(jnp.float32)
-        return (input_grad, grad_uf, grad_us, grad_df, grad_ds)
     wide_sum = (
         lax.psum_scatter(grad_us, "dp", scatter_dimension=1, tiled=True),
         lax.psum_scatter(grad_df, "dp", scatter_dimension=1, tiled=True),
@@ -472,6 +548,58 @@
     grad_uf = square_sum[0] * factor
     grad_ds = square_sum[1] * factor
     return (input_grad, grad_uf, grad_us, grad_df, grad_ds)
+
+
+def per_device(tokens, up_first, up_second, down_first, down_second, cotangent):
+    size, spread = lax.axis_size("dp"), lax.axis_size("blk")
+    tok_rows = tokens.shape[0]
+    local_blocks, _, block_size = up_first.shape
+    weights = (down_second, up_first, up_second, down_first)
+    tiled = (
+        size % SIDE == 0
+        and size > SIDE
+        and spread > 1
+        and all(w.shape[1] % 16 == 0 for w in weights)
+        and block_size % (16 * spread) == 0
+        and block_size == local_blocks * spread
+    )
+    if not tiled:
+        return by_collectives(tokens, up_first, up_second, down_first, down_second, cotangent)
+    factor = 1.0 / math.sqrt(tok_rows * size)
+    full_ds, full_uf, full_us, full_df, back_down, moved_up = gather_rows(
+        weights, tokens, cotangent, size
+    )
+    inputs_b = tokens.reshape(tok_rows, local_blocks, block_size)
+    upstream = cotangent.reshape(tok_rows, local_blocks, block_size)
+    pre_act = jnp.einsum("bjt,jbk->tjk", moved_up, full_us, preferred_element_type=jnp.float32)
+    hidden = activation(pre_act).astype(jnp.bfloat16)
+    hidden_grad = jnp.einsum("jbt,bij->tbi", back_down, full_df, preferred_element_type=jnp.float32)
+    _, pull_back = jax.vjp(activation, pre_act)
+    pre_grad = pull_back(hidden_grad)[0].astype(jnp.bfloat16)
+    first_down = jnp.einsum(
+        "tbi,bij->tbj", hidden, full_df, preferred_element_type=jnp.float32
+    ).astype(jnp.bfloat16)
+    moved_down = permute_forward(first_down, None)[0]
+    back_up = permute_backward(pre_grad, full_us)
+    grad_ds = jnp.einsum("tbj,tjk->jbk", moved_down, upstream, preferred_element_type=jnp.float32)
+    grad_df = jnp.einsum("tbi,jbt->bij", hidden, back_down, preferred_element_type=jnp.float32)
+    grad_us = jnp.einsum("bjt,tjk->jbk", moved_up, pre_grad, preferred_element_type=jnp.float32)
+    grad_uf = jnp.einsum("tbi,tbj->bij", inputs_b, back_up, preferred_element_type=jnp.float32)
+    input_grad = jnp.einsum(
+        "tbj,bij->tbi", back_up, full_uf, preferred_element_type=jnp.float32
+    ).astype(jnp.bfloat16)
+    input_grad = input_grad.reshape(tok_rows, local_blocks * block_size)
+    grads = (grad_ds, grad_uf, grad_us, grad_df)
+    grad_ds, grad_uf, grad_us, grad_df = reduce_rows(
+        tuple(g.astype(jnp.bfloat16) for g in grads), 2, size, factor
+    )
+    return (
+        input_grad,
+        grad_uf.astype(jnp.float32),
+        grad_us,
+        grad_df,
+        grad_ds.astype(jnp.float32),
+    )
 
 
 def solution(mesh):

time: 269 us -> 238 us (0.88)
  waiting for transfers between devices: 36.4 us -> 11.2 us
  Pallas kernels: 170 us -> 180 us
  starting transfers between devices: 16.5 us -> 7.94 us
  local copies, waits for them, and re-layouts: 15.6 us -> 11.4 us
  matrix products: 26 us -> 23.1 us
    all_to_all x2 -> x1, waiting for transfers between devices: 19.6 us -> 3.7 us  [permute_forward(): lax.all_to_all(lower, 'blk', split_axis=2, concat_axis=1, tiled=True)]
    pallas_call x1, Pallas kernels: 73.6 us -> 83.3 us  [gather_rows(): pl.pallas_call(functools.partial(gather_kernel, size), out_shape=tuple((j...]
    all_to_all x2 -> x1, waiting for transfers between devices: 16.8 us -> 7.48 us  [permute_backward(): lax.all_to_all(spread, 'blk', split_axis=1, concat_axis=2, tiled=True)]
    all_to_all x2 -> x1, starting transfers between devices: 8.5 us -> 3.52 us  [permute_forward(): lax.all_to_all(lower, 'blk', split_axis=2, concat_axis=1, tiled=True)]
    dot_general x5 -> x4, matrix products: 13.2 us -> 16.7 us  [the longest x1 6.42 us: per_device(): jnp.einsum('jbt,bij->tbi', back_down, full_df, preferred_element_type=jnp...]
    all_to_all x2 -> x1, starting transfers between devices: 7.96 us -> 4.43 us  [permute_backward(): lax.all_to_all(spread, 'blk', split_axis=1, concat_axis=2, tiled=True)]
    unnamed x25 -> x23, local copies, waits for them, and re-layouts: 3.55 us -> 6.63 us
    dot_general x1, matrix products: 4.88 us -> 1.92 us  [per_device(): jnp.einsum('tbi,bij->tbj', hidden, full_df, preferred_element_type=jnp.fl...]
  transfers between devices with their start and end apart: 4 -> 2, of which waited for: 4 -> 2; matrix products, arithmetic and copies ran while one was open for 8% -> 7% of each run, Pallas kernels for 0% -> 0%
where the time goes in v2:
time: 238 us
  Pallas kernels  180 us (76%)
  matrix products  23.1 us (10%)
  local copies, waits for them, and re-layouts  11.4 us (5%)
  waiting for transfers between devices  11.2 us (5%)
  starting transfers between devices  7.94 us (3%)
  other arithmetic  3.13 us (1%)
    pallas_call x1, Pallas kernels, reduce_rows(): pl.pallas_call(functools.partial(reduce_kernel, size, scale, shared), out...  97.1 us
    pallas_call x1, Pallas kernels, gather_rows(): pl.pallas_call(functools.partial(gather_kernel, size), out_shape=tuple((j...  83.3 us
    all_to_all x1, waiting for transfers between devices, permute_backward(): lax.all_to_all(spread, 'blk', split_axis=1, concat_axis=2, tiled=True)  7.48 us
    unnamed x23, local copies, waits for them, and re-layouts  6.63 us
    dot_general x1, matrix products, per_device(): jnp.einsum('jbt,bij->tbi', back_down, full_df, preferred_element_type=jnp...  6.42 us
    dot_general x1, matrix products, per_device(): jnp.einsum('tbi,jbt->bij', hidden, back_down, preferred_element_type=jnp....  5.3 us
  transfers between devices with their start and end apart: 2, of which 2 were waited for; matrix products, arithmetic and copies ran while one was open for 7% of the time, Pallas kernels for 0%

profile of v2, /device:TPU:0, one launch (start us, length us, event | category | flops | bytes accessed | tf_op | source)
XLA Modules:
  0.0 237.9 jit_solution(16246714776989041289)
XLA Ops:
  0.6 0.9 copy-done
  1.6 0.9 copy-done.1
  2.5 0.9 copy-done.2
  3.4 0.9 copy-done.3
  4.3 83.3 %gather_rows.1 = (bf16[32,128,128]{2,1,0:T(8,128)(2,1)}, bf16[32,128,128]{2,1,0:T(8,128)(2,1)S(1)}, bf16[32,128,256]{2,1,0:T(8,128)(2,1)}, bf16[32,256,128]{2,1,...) custom-call(bf16[32,16,128]{2,1,0:T(8,128)(2,1)S(1)} %copy-done.2, ...), custom_call_target="tpu_custom_call" | custom-call | tf_op jit(solution)/shard_map/gather_rows/pallas_call | solution.py:275
  87.6 2.9 %fusion.19 = f32[32,256,128]{2,1,0:T(8,128)S(1)} fusion(bf16[32,128,256]{2,1,0:T(8,128)(2,1)} %get-tuple-element.15, bf16[128,32,128]{2,1,0:T(8,128)(2,1)} %get-tuple-element.18), kind=kOutput, calls=%fused_computation.31 | convolution fusion | flops 268435456 | bytes 7340032 | tf_op jit(solution)/shard_map/bjt,jbk->tjk/dot_general | solution.py:574
  90.5 1.9 fusion.12
  92.4 1.6 copy.69
  94.1 3.5 %all-to-all-start.1 = ((bf16[128,32,128]{0,1,2:T(8,128)(2,1)}), bf16[128,32,128]{0,1,2:T(8,128)(2,1)S(1)}, u32[]{:S(2)}, u32[]{:S(2)}) async-start(bf16[128,32,128]{0,1,2:T(8,128)(2,1)} %copy.69), calls=%async_computation.1 | async-start | bytes 2097152 | tf_op jit(solution)/shard_map/all_to_all | solution.py:495
  97.6 6.4 %fusion.6 = bf16[128,32,256]{0,2,1:T(8,128)(2,1)S(1)} fusion(f32[32,256,128]{2,1,0:T(8,128)} %copy-done.6, bf16[32,256,128]{2,1,0:T(8,128)(2,1)} %get-tuple-element.16, bf16[128,32,128]{2,1,0:T(8,128)(2,1)S(1)} %get-tuple-element.17), kind=kOutput, calls=%fused_computation.8 | convolution fusion | flops 289406976 | bytes 9437184 | tf_op jit(solution)/shard_map/jbt,bij->tbi/dot_general | solution.py:576
  104.8 1.6 copy.64
  106.4 2.2 convolution_convert_fusion.1.refs_2_
  108.6 3.7 %all-to-all-done.1 = bf16[128,32,128]{0,1,2:T(8,128)(2,1)S(1)} async-done(((bf16[128,32,128]{0,1,2:T(8,128)(2,1)}), bf16[128,32,128]{0,1,2:T(8,128)(2,1)S(1)}, u32[]{:S(2)}, u32[]{:S(2)}) %all-to-all-start.1) | async-done | bytes 1048608 | tf_op jit(solution)/shard_map/all_to_all | solution.py:495
  112.3 4.4 %all-to-all-start = ((bf16[128,128,32]{0,2,1:T(8,128)(2,1)}), bf16[128,128,32]{0,2,1:T(8,128)(2,1)}, u32[]{:S(2)}, u32[]{:S(2)}) async-start(bf16[128,128,32]{0,2,1:T(8,128)(2,1)} %copy.64), calls=%async_computation | async-start | bytes 2097152 | tf_op jit(solution)/shard_map/all_to_all | solution.py:502
  116.7 5.3 %convolution_convert_fusion.refs_3_ = bf16[32,256,128]{2,1,0:T(8,128)(2,1)} fusion(bf16[128,32,128]{2,1,0:T(8,128)(2,1)S(1)} %get-tuple-element.17, f32[32,256,128]{2,1,0:T(8,128)} %copy-done.6), kind=kOutput, calls=%fused_computation.16 | convolution fusion | flops 278921216 | bytes 7340032 | tf_op jit(solution)/shard_map/tbi,jbt->bij/dot_general | solution.py:585
  122.2 1.4 convolution_convert_fusion.3.refs_0_
  123.6 7.5 %all-to-all-done = bf16[128,128,32]{0,2,1:T(8,128)(2,1)} async-done(((bf16[128,128,32]{0,2,1:T(8,128)(2,1)}), bf16[128,128,32]{0,2,1:T(8,128)(2,1)}, u32[]{:S(2)}, u32[]{:S(2)}) %all-to-all-start) | async-done | bytes 1048608 | tf_op jit(solution)/shard_map/all_to_all | solution.py:502
  131.1 1.4 copy.65
  132.4 1.9 fusion.13.refs_1_
  134.8 1.3 copy.77
  136.1 97.1 %reduce_rows.1 = (bf16[32,128,128]{2,1,0:T(8,128)(2,1)S(1)}, bf16[32,128,128]{2,1,0:T(8,128)(2,1)S(1)}, f32[32,16,256]{2,1,0:T(8,128)S(1)}, f32[32,32,128]{2,1,0:T(8,128)S(1)}) custom-call(bf16[32,128,128]{2,1,0:T(8,128)(2,1)} %convolution_convert_fusion.3.refs_0_, bf16[32,128,128]{2,1,0:T(8,128)(2,1)} %fusion.13.refs_1_, ...), custom_call_target="tpu_custom_call" | custom-call | tf_op jit(solution)/shard_map/reduce_rows/pallas_call | solution.py:458
  233.2 1.6 convert_element_type.57
  234.8 1.6 convert_element_type.58
  236.3 0.8 copy.105
  (20 shorter events, 2.1 us)
Async XLA Ops:
  0.6 1.0 copy-start
  1.6 0.9 copy-start.1
  2.5 0.9 copy-start.2
  3.4 0.9 copy-start.3
  87.6 2.9 %copy-start.9 = (bf16[32,256,128]{2,1,0:T(8,128)(2,1)S(1)}, bf16[32,256,128]{2,1,0:T(8,128)(2,1)}, u32[]{:S(2)}) copy-start(bf16[32,256,128]{2,1,0:T(8,128)(2,1)} %get-tuple-element.16) | copy-start | bytes 6291460
  90.5 2.0 copy-start.6
  94.1 18.2 %all-to-all-start.1 = ((bf16[128,32,128]{0,1,2:T(8,128)(2,1)}), bf16[128,32,128]{0,1,2:T(8,128)(2,1)S(1)}, u32[]{:S(2)}, u32[]{:S(2)}) async-start(bf16[128,32,128]{0,1,2:T(8,128)(2,1)} %copy.69), calls=%async_computation.1 | async-start | bytes 2097152 | tf_op jit(solution)/shard_map/all_to_all | solution.py:495
  97.6 6.4 %copy-start.4 = (bf16[32,128,256]{2,1,0:T(8,128)(2,1)S(1)}, bf16[32,128,256]{2,1,0:T(8,128)(2,1)}, u32[]{:S(2)}) copy-start(bf16[32,128,256]{2,1,0:T(8,128)(2,1)} %get-tuple-element.15) | copy-start | bytes 6291460
  104.1 2.4 copy-start.5
  112.3 18.8 %all-to-all-start = ((bf16[128,128,32]{0,2,1:T(8,128)(2,1)}), bf16[128,128,32]{0,2,1:T(8,128)(2,1)}, u32[]{:S(2)}, u32[]{:S(2)}) async-start(bf16[128,128,32]{0,2,1:T(8,128)(2,1)} %copy.64), calls=%async_computation | async-start | bytes 2097152 | tf_op jit(solution)/shard_map/all_to_all | solution.py:502
  116.7 5.4 %copy-start.7 = (bf16[128,4096]{1,0:T(8,128)(2,1)S(1)}, bf16[128,4096]{1,0:T(8,128)(2,1)}, u32[]{:S(2)}) copy-start(bf16[128,4096]{1,0:T(8,128)(2,1)} %refs_5_.1) | copy-start | bytes 3145732
  122.0 10.4 %copy-start.8 = (bf16[128,4096]{1,0:T(8,128)(2,1)S(1)}, bf16[128,4096]{1,0:T(8,128)(2,1)}, u32[]{:S(2)}) copy-start(bf16[128,4096]{1,0:T(8,128)(2,1)} %refs_4_.1) | copy-start | bytes 3145732

commit v3 on v2

--- a/solution.py
+++ b/solution.py
@@ -173,18 +173,29 @@
 
 
 class Exchange:
-    def __init__(self, made, out, local_sem, sends, recv):
+    def __init__(self, made, out, local_sem, sends, recv, leading=False):
+        self.leading = leading
         self.made, self.out, self.local_sem, self.sends, self.recv = made, out, local_sem, sends, recv
         self.count = lax.axis_size("blk")
-        self.blocks = made.shape[0]
-        self.part = made.shape[1] // self.count
+        self.blocks = made.shape[1 if leading else 0]
+        self.part = made.shape[0 if leading else 1] // self.count
         self.me = lax.axis_index("blk")
+
+    def _piece(self, target):
+        if self.leading:
+            return self.made.at[pl.ds(target * self.part, self.part)]
+        return rows_of(self.made, target, self.part)
+
+    def _place(self):
+        if self.leading:
+            return rows_of(self.out, self.me, self.blocks)
+        return self.out.at[pl.ds(self.me * self.blocks, self.blocks)]
 
     def _copy(self, hop):
         target = lax.rem(self.me + hop, self.count)
         return pltpu.make_async_remote_copy(
-            src_ref=rows_of(self.made, target, self.part),
-            dst_ref=self.out.at[pl.ds(self.me * self.blocks, self.blocks)],
+            src_ref=self._piece(target),
+            dst_ref=self._place(),
             send_sem=self.sends.at[hop],
             recv_sem=self.recv.at[hop],
             device_id={"blk": target},
@@ -192,11 +203,7 @@
         )
 
     def _local(self):
-        return pltpu.make_async_copy(
-            rows_of(self.made, self.me, self.part),
-            self.out.at[pl.ds(self.me * self.blocks, self.blocks)],
-            self.local_sem,
-        )
+        return pltpu.make_async_copy(self._piece(self.me), self._place(), self.local_sem)
 
     def begin(self):
         for hop in range(1, self.count):
@@ -404,13 +411,17 @@
             pl.when(p.z >= distance)(lambda: self._down(p.z - distance).wait_send())
 
 
-def reduce_kernel(size, scale, shared, *refs):
-    count = 4
-    grads, outs = refs[:count], refs[count : 2 * count]
-    rest = refs[2 * count :]
+def reduce_kernel(size, scale, *refs):
+    count, shared = 4, 2
+    grad_us, grad_df, made_down, made_up, tokens, upstream, full_uf = refs[:7]
+    input_grad, outs = refs[7], refs[8 : 8 + count]
+    grad_ds, grad_uf, moved_down, moved_up = refs[8 + count : 12 + count]
+    local_blk, sends_blk, recv_blk = refs[12 + count : 15 + count]
+    rest = refs[15 + count :]
     crosses, lows, highs, stages = (rest[k * count : (k + 1) * count] for k in range(4))
     finals = rest[4 * count : 4 * count + shared]
     sems, local, sends, recv = rest[4 * count + shared :]
+    grads = (grad_ds, grad_uf, grad_us, grad_df)
     place = Place(size)
     greet(place)
     reduces = [
@@ -428,17 +439,72 @@
         )
         for a in range(shared)
     ]
+    down = Exchange(
+        made_down, moved_down, local_blk.at[0], sends_blk.at[0], recv_blk.at[0], True
+    )
+    up = Exchange(made_up, moved_up, local_blk.at[1], sends_blk.at[1], recv_blk.at[1], True)
+    blocks, width = grad_uf.shape[0], grad_uf.shape[1]
+
+    def columns_of(block):
+        return pl.ds(pl.multiple_of(block * width, width), width)
+
+    def make_ds():
+        down.finish()
+
+        @pl.loop(0, blocks, unroll=2)
+        def _(block):
+            grad_ds[block] = jnp.dot(
+                moved_down[block], upstream[:, columns_of(block)],
+                preferred_element_type=jnp.float32,
+            ).astype(jnp.bfloat16)
+
+        for distance in range(place.depth - 1, -1, -1):
+            reduces[0].send_across(distance)
+
+    def make_uf():
+        up.finish()
+
+        @pl.loop(0, blocks, unroll=2)
+        def _(block):
+            product = jnp.dot(
+                moved_up[block], tokens[:, columns_of(block)],
+                preferred_element_type=jnp.float32,
+            )
+            grad_uf[block] = product.T.astype(jnp.bfloat16)
+
+        for distance in range(place.depth - 1, -1, -1):
+            reduces[1].send_across(distance)
+
+    def make_input_grad():
+        @pl.loop(0, blocks, unroll=2)
+        def _(block):
+            product = jnp.dot(
+                full_uf[block], moved_up[block], preferred_element_type=jnp.float32
+            )
+            input_grad[:, columns_of(block)] = product.T.astype(jnp.bfloat16)
+
+    down.begin()
+    up.begin()
     for distance in range(place.depth - 1, -1, -1):
-        for reduce in reduces:
+        for reduce in reduces[shared:]:
             reduce.send_across(distance)
+    pending = [make_ds, make_uf]
     for distance in range(place.depth - 1, 0, -1):
-        for reduce in reduces:
+        for reduce in reduces[shared:]:
+            reduce.step(distance)
+        if pending:
+            pending.pop(0)()
+    for make in pending:
+        make()
+    for distance in range(place.depth - 1, 0, -1):
+        for reduce in reduces[:shared]:
             reduce.step(distance)
     for a in range(shared):
         reduces[a].last()
         gathers[a].begin()
     for a in range(shared, count):
         reduces[a].last()
+    make_input_grad()
     for distance in range(1, place.depth):
         for gather in gathers:
             gather.step(distance)
@@ -448,24 +514,30 @@
         reduce.finish()
 
 
-def reduce_rows(grads, shared, size, scale):
-    depth = size // SIDE
+def reduce_rows(grad_us, grad_df, made_down, made_up, tokens, upstream, full_uf, size, scale):
+    depth, spread, shared = size // SIDE, lax.axis_size("blk"), 2
+    square = jax.ShapeDtypeStruct(full_uf.shape, jnp.bfloat16)
+    grads = (square, square, grad_us, grad_df)
     parts = [(g.shape[0], g.shape[1] // size, g.shape[2]) for g in grads]
     slots = [pltpu.VMEM((depth,) + part, jnp.bfloat16) for part in parts]
+    moved = (made_down.shape[0] // spread, made_down.shape[1] * spread, made_down.shape[2])
     vmem = pl.BlockSpec(memory_space=pltpu.VMEM)
     anywhere = pl.BlockSpec(memory_space=pl.ANY)
     count = len(grads)
     return pl.pallas_call(
-        functools.partial(reduce_kernel, size, scale, shared),
-        out_shape=tuple(
-            jax.ShapeDtypeStruct(g.shape, jnp.bfloat16)
-            if a < shared
-            else jax.ShapeDtypeStruct(parts[a], jnp.float32)
-            for a, g in enumerate(grads)
-        ),
-        in_specs=[vmem] * count,
-        out_specs=tuple(anywhere if a < shared else vmem for a in range(count)),
-        scratch_shapes=slots * 4
+        functools.partial(reduce_kernel, size, scale),
+        out_shape=(jax.ShapeDtypeStruct(tokens.shape, jnp.bfloat16), square, square)
+        + tuple(jax.ShapeDtypeStruct(part, jnp.float32) for part in parts[shared:]),
+        in_specs=[vmem] * 7,
+        out_specs=(vmem, anywhere, anywhere, vmem, vmem),
+        scratch_shapes=[pltpu.VMEM(square.shape, jnp.bfloat16)] * 2
+        + [pltpu.VMEM(moved, jnp.bfloat16)] * 2
+        + [
+            pltpu.SemaphoreType.DMA((2,)),
+            pltpu.SemaphoreType.DMA((2, spread)),
+            pltpu.SemaphoreType.DMA((2, spread)),
+        ]
+        + slots * 4
         + [pltpu.VMEM(parts[a], jnp.bfloat16) for a in range(shared)]
         + [
             pltpu.SemaphoreType.DMA((count, 6, depth)),
@@ -477,7 +549,7 @@
             collective_id=1, has_side_effects=True, vmem_limit_bytes=VMEM_BYTES
         ),
         name="reduce_rows",
-    )(*grads)
+    )(grad_us, grad_df, made_down, made_up, tokens, upstream, full_uf)
 
 
 def activation(values):
@@ -562,6 +634,7 @@
         and all(w.shape[1] % 16 == 0 for w in weights)
         and block_size % (16 * spread) == 0
         and block_size == local_blocks * spread
+        and local_blocks % 16 == 0
     )
     if not tiled:
         return by_collectives(tokens, up_first, up_second, down_first, down_second, cotangent)
@@ -569,29 +642,29 @@
     full_ds, full_uf, full_us, full_df, back_down, moved_up = gather_rows(
         weights, tokens, cotangent, size
     )
-    inputs_b = tokens.reshape(tok_rows, local_blocks, block_size)
-    upstream = cotangent.reshape(tok_rows, local_blocks, block_size)
     pre_act = jnp.einsum("bjt,jbk->tjk", moved_up, full_us, preferred_element_type=jnp.float32)
     hidden = activation(pre_act).astype(jnp.bfloat16)
     hidden_grad = jnp.einsum("jbt,bij->tbi", back_down, full_df, preferred_element_type=jnp.float32)
     _, pull_back = jax.vjp(activation, pre_act)
     pre_grad = pull_back(hidden_grad)[0].astype(jnp.bfloat16)
     first_down = jnp.einsum(
-        "tbi,bij->tbj", hidden, full_df, preferred_element_type=jnp.float32
+        "tbi,bij->jbt", hidden, full_df, preferred_element_type=jnp.float32
     ).astype(jnp.bfloat16)
-    moved_down = permute_forward(first_down, None)[0]
-    back_up = permute_backward(pre_grad, full_us)
-    grad_ds = jnp.einsum("tbj,tjk->jbk", moved_down, upstream, preferred_element_type=jnp.float32)
+    back_up = jnp.einsum(
+        "tjk,jbk->bjt", pre_grad, full_us, preferred_element_type=jnp.float32
+    ).astype(jnp.bfloat16)
     grad_df = jnp.einsum("tbi,jbt->bij", hidden, back_down, preferred_element_type=jnp.float32)
     grad_us = jnp.einsum("bjt,tjk->jbk", moved_up, pre_grad, preferred_element_type=jnp.float32)
-    grad_uf = jnp.einsum("tbi,tbj->bij", inputs_b, back_up, preferred_element_type=jnp.float32)
-    input_grad = jnp.einsum(
-        "tbj,bij->tbi", back_up, full_uf, preferred_element_type=jnp.float32
-    ).astype(jnp.bfloat16)
-    input_grad = input_grad.reshape(tok_rows, local_blocks * block_size)
-    grads = (grad_ds, grad_uf, grad_us, grad_df)
-    grad_ds, grad_uf, grad_us, grad_df = reduce_rows(
-        tuple(g.astype(jnp.bfloat16) for g in grads), 2, size, factor
+    input_grad, grad_ds, grad_uf, grad_us, grad_df = reduce_rows(
+        grad_us.astype(jnp.bfloat16),
+        grad_df.astype(jnp.bfloat16),
+        first_down,
+        back_up,
+        tokens,
+        cotangent,
+        full_uf,
+        size,
+        factor,
     )
     return (
         input_grad,

time: 238 us -> 220 us (0.924)
  waiting for transfers between devices: 11.2 us -> 0 us
  Pallas kernels: 180 us -> 190 us
  matrix products: 23.1 us -> 14.8 us
  starting transfers between devices: 7.94 us -> 0 us
    all_to_all x2 -> x0, waiting for transfers between devices: 11.2 us -> none  [the longest x1 7.48 us: permute_backward(): lax.all_to_all(spread, 'blk', split_axis=1, concat_axis=2, tiled=True)]
    pallas_call x1, Pallas kernels: 97.1 us -> 106 us  [reduce_rows(): pl.pallas_call(functools.partial(reduce_kernel, size, scale), out_shape=(...]
    all_to_all x2 -> x0, starting transfers between devices: 7.94 us -> none  [the longest x1 4.43 us: permute_backward(): lax.all_to_all(spread, 'blk', split_axis=1, concat_axis=2, tiled=True)]
    dot_general x5 -> x2, matrix products: 6.36 us -> 2.63 us  [the longest x1 1.93 us: per_device(): jnp.einsum('tbi,bij->jbt', hidden, full_df, preferred_element_type=jnp.fl...]
    dot_general x1, matrix products: 6.42 us -> 3.9 us  [per_device(): jnp.einsum('jbt,bij->tbi', back_down, full_df, preferred_element_type=jnp...]
    unnamed x23 -> x19, local copies, waits for them, and re-layouts: 6.63 us -> 6.79 us
  transfers between devices with their start and end apart: 2 -> 0, of which waited for: 2 -> 0; matrix products, arithmetic and copies ran while one was open for 7% -> 0% of each run, Pallas kernels for 0% -> 0%
where the time goes in v3:
time: 220 us; the launch traced here: 219 us
  Pallas kernels  190 us (86%)
  matrix products  14.8 us (7%)
  local copies, waits for them, and re-layouts  9.46 us (4%)
  other arithmetic  4.35 us (2%)
    pallas_call x1, Pallas kernels, reduce_rows(): pl.pallas_call(functools.partial(reduce_kernel, size, scale), out_shape=(...  106 us
    pallas_call x1, Pallas kernels, gather_rows(): pl.pallas_call(functools.partial(gather_kernel, size), out_shape=tuple((j...  83.2 us
    unnamed x19, local copies, waits for them, and re-layouts  6.79 us

profile of v3, /device:TPU:0, one launch (start us, length us, event | category | flops | bytes accessed | tf_op | source)
XLA Modules:
  0.0 219.0 jit_solution(8112191712375267464)
XLA Ops:
  0.6 0.0 copy-start.1
  0.6 0.9 copy-done.1
  1.6 0.9 copy-done.2
  2.5 0.9 copy-done.3
  3.4 0.9 copy-done.4
  4.3 83.2 %gather_rows.1 = (bf16[32,128,128]{2,1,0:T(8,128)(2,1)}, bf16[32,128,128]{2,1,0:T(8,128)(2,1)S(1)}, bf16[32,128,256]{2,1,0:T(8,128)(2,1)}, bf16[32,256,128]{2,1,...) custom-call(bf16[32,16,128]{2,1,0:T(8,128)(2,1)S(1)} %copy-done.3, ...), custom_call_target="tpu_custom_call" | custom-call | tf_op jit(solution)/shard_map/gather_rows/pallas_call | solution.py:282
  87.6 0.0 copy-start
  87.6 0.0 copy-start.7
  87.6 3.1 %fusion.13 = f32[32,256,128]{2,1,0:T(8,128)S(1)} fusion(bf16[32,128,256]{2,1,0:T(8,128)(2,1)} %get-tuple-element.18, bf16[128,32,128]{2,1,0:T(8,128)(2,1)} %get-tuple-element.15), kind=kOutput, calls=%fused_computation.22 | convolution fusion | flops 268435456 | bytes 7340032 | tf_op jit(solution)/shard_map/bjt,jbk->tjk/dot_general | solution.py:645
  90.7 0.0 copy-done.7
  90.8 1.9 fusion.18
  92.7 0.0 copy-done
  92.7 3.9 %fusion.6 = bf16[128,32,256]{0,2,1:T(8,128)(2,1)S(1)} fusion(f32[32,256,128]{2,1,0:T(8,128)S(1)} %fusion.13, bf16[32,256,128]{2,1,0:T(8,128)(2,1)S(1)} %copy-done.7, bf16[128,32,128]{2,1,0:T(8,128)(2,1)S(1)} %get-tuple-element.17), kind=kOutput, calls=%fused_computation.8 | convolution fusion | flops 289406976 | bytes 9437184 | tf_op jit(solution)/shard_map/jbt,bij->tbi/dot_general | solution.py:647
  96.6 3.1 %convolution_convert_fusion.refs_1_ = bf16[32,256,128]{2,1,0:T(8,128)(2,1)} fusion(bf16[128,32,128]{2,1,0:T(8,128)(2,1)S(1)} %get-tuple-element.17, f32[32,256,128]{2,1,0:T(8,128)S(1)} %fusion.13), kind=kOutput, calls=%fused_computation.18 | convolution fusion | flops 278921216 | bytes 7340032 | tf_op jit(solution)/shard_map/tbi,jbt->bij/dot_general | solution.py:656
  99.7 0.7 fusion.21
  100.4 0.5 copy-done.6
  101.0 2.0 convolution_convert_fusion.1.refs_0_
  103.0 2.7 %fusion.11 = (bf16[128,32,128]{2,1,0:T(8,128)(2,1)}, bf16[128,32,128]{2,1,0:T(8,128)(2,1)}) fusion(bf16[32,128,128]{2,1,0:T(8,128)(2,1)S(1)} %fusion.18, bf16[32,128,128]{2,1,0:T(8,128)(2,1)S(1)} %fusion.21), kind=kLoop, calls=%fused_computation.20 | loop fusion | bytes 4194304 | tf_op jit(solution)/shard_map/convert_element_type | solution.py:652
  105.7 106.4 %reduce_rows.1 = (bf16[128,4096]{1,0:T(8,128)(2,1)S(1)}, bf16[32,128,128]{2,1,0:T(8,128)(2,1)S(1)}, bf16[32,128,128]{2,1,0:T(8,128)(2,1)}, f32[32,16,256]{2,1,0:T(8,128)S(1)}, f32[32,32,128]{2,1,0:T(8,128)S(1)}) custom-call(bf16[32,128,256]{2,1,0:T(8,128)(2,1)} %convolution_convert_fusion.1.refs_0_, bf16[32,256,128]{2,1,0:T(8,128)(2,1)} %convolution_convert_fusion.refs_1_, ...), custom_call_target="tpu_custom_call" | custom-call | tf_op jit(solution)/shard_map/reduce_rows/pallas_call | solution.py:527
  212.1 2.8 %convert_element_type.36 = f32[32,128,128]{2,1,0:T(8,128)} convert(bf16[32,128,128]{2,1,0:T(8,128)(2,1)} %get-tuple-element.21) | non-fusion elementwise | flops 524288 | bytes 3145728 | tf_op jit(solution)/shard_map/convert_element_type | solution.py:671
  214.9 1.6 convert_element_type.37
  216.4 1.0 copy.44
  217.4 0.8 copy.45
  218.2 0.8 copy.46
  (6 shorter events, 0.0 us)
Async XLA Ops:
  0.6 1.0 copy-start.1
  1.6 0.9 copy-start.2
  2.5 0.9 copy-start.3
  3.4 0.9 copy-start.4
  87.6 5.1 %copy-start = (bf16[32,128,128]{2,1,0:T(8,128)(2,1)}, bf16[32,128,128]{2,1,0:T(8,128)(2,1)S(1)}, u32[]{:S(2)}) copy-start(bf16[32,128,128]{2,1,0:T(8,128)(2,1)S(1)} %get-tuple-element.19.refs_6_) | copy-start | bytes 3145732
  87.6 3.1 %copy-start.7 = (bf16[32,256,128]{2,1,0:T(8,128)(2,1)S(1)}, bf16[32,256,128]{2,1,0:T(8,128)(2,1)}, u32[]{:S(2)}) copy-start(bf16[32,256,128]{2,1,0:T(8,128)(2,1)} %get-tuple-element.16) | copy-start | bytes 6291460
  96.6 3.1 %copy-start.5 = (bf16[32,128,256]{2,1,0:T(8,128)(2,1)S(1)}, bf16[32,128,256]{2,1,0:T(8,128)(2,1)}, u32[]{:S(2)}) copy-start(bf16[32,128,256]{2,1,0:T(8,128)(2,1)} %get-tuple-element.18) | copy-start | bytes 6291460
  99.7 1.2 copy-start.6

commit v4 on v3

--- a/solution.py
+++ b/solution.py
@@ -233,15 +233,19 @@
     down = Exchange(back, moved_down, local_blk.at[0], sends_blk.at[0], recv_blk.at[0])
     up = Exchange(first, moved_up, local_blk.at[1], sends_blk.at[1], recv_blk.at[1])
     blocks, width = first.shape[0], first.shape[1]
-    for gather in gathers:
+    for gather in gathers[:2]:
         gather.begin()
     gathers[0].begin_wide()
+    late = list(gathers[2:])
     for distance in range(1, place.depth):
         for gather in gathers[:2]:
             gather.step(distance)
-        if distance < place.depth - 1:
-            for gather in gathers[2:]:
-                gather.step(distance)
+        if late:
+            late.pop(0).begin()
+    for gather in late:
+        gather.begin()
+    for gather in gathers[2:]:
+        gather.step(1)
     gathers[0].finish()
 
     @pl.loop(0, blocks, unroll=2)
@@ -253,8 +257,9 @@
         ).astype(jnp.bfloat16)
 
     down.begin()
-    for gather in gathers[2:]:
-        gather.step(place.depth - 1)
+    for distance in range(2, place.depth - 1):
+        for gather in gathers[2:]:
+            gather.step(distance)
     gathers[1].finish()
 
     @pl.loop(0, blocks, unroll=2)
@@ -266,6 +271,9 @@
         first[block] = product.T.astype(jnp.bfloat16)
 
     up.begin()
+    for gather in gathers[2:]:
+        if place.depth > 2:
+            gather.step(place.depth - 1)
     for gather in gathers[2:]:
         gather.finish()
     down.finish()
@@ -435,7 +443,7 @@
     gathers = [
         Gather(
             place, finals[a], outs[a], finals[a].shape[1],
-            local.at[a], sends.at[a], recv.at[a], False,
+            local.at[a], sends.at[a], recv.at[a], a == 0,
         )
         for a in range(shared)
     ]
@@ -485,29 +493,38 @@
 
     down.begin()
     up.begin()
-    for distance in range(place.depth - 1, -1, -1):
+    far = range(place.depth - 1, 1, -1)
+    for distance in far:
         for reduce in reduces[shared:]:
             reduce.send_across(distance)
     pending = [make_ds, make_uf]
-    for distance in range(place.depth - 1, 0, -1):
+    for distance in far:
         for reduce in reduces[shared:]:
             reduce.step(distance)
         if pending:
             pending.pop(0)()
     for make in pending:
         make()
+    for distance in (1, 0):
+        for reduce in reduces[shared:]:
+            reduce.send_across(distance)
     for distance in range(place.depth - 1, 0, -1):
         for reduce in reduces[:shared]:
             reduce.step(distance)
     for a in range(shared):
         reduces[a].last()
         gathers[a].begin()
-    for a in range(shared, count):
-        reduces[a].last()
-    make_input_grad()
-    for distance in range(1, place.depth):
+    for reduce in reduces[shared:]:
+        reduce.step(1)
+    gathers[0].begin_wide()
+    for gather in gathers:
+        gather.step(1)
+    for reduce in reduces[shared:]:
+        reduce.last()
+    for distance in range(2, place.depth):
         for gather in gathers:
             gather.step(distance)
+    make_input_grad()
     for gather in gathers:
         gather.finish()
     for reduce in reduces:

time: 220 us -> 218 us (level)
    pallas_call x1, Pallas kernels: 83.2 us -> 78.5 us  [gather_rows(): pl.pallas_call(functools.partial(gather_kernel, size), out_shape=tuple((j...]
    pallas_call x1, Pallas kernels: 106 us -> 110 us  [reduce_rows(): pl.pallas_call(functools.partial(reduce_kernel, size, scale), out_shape=(...]
where the time goes in v4:
time: 218 us; the launch traced here: 217 us
  Pallas kernels  188 us (86%)
  matrix products  14.8 us (7%)
  local copies, waits for them, and re-layouts  9.46 us (4%)
  other arithmetic  4.35 us (2%)
    pallas_call x1, Pallas kernels, reduce_rows(): pl.pallas_call(functools.partial(reduce_kernel, size, scale), out_shape=(...  110 us
    pallas_call x1, Pallas kernels, gather_rows(): pl.pallas_call(functools.partial(gather_kernel, size), out_shape=tuple((j...  78.5 us
    unnamed x19, local copies, waits for them, and re-layouts  6.79 us

profile of v4, /device:TPU:0, one launch (start us, length us, event | category | flops | bytes accessed | tf_op | source)
XLA Modules:
  0.0 217.5 jit_solution(9509709502342591375)
XLA Ops:
  0.6 0.0 copy-start.1
  0.6 0.9 copy-done.1
  1.6 0.9 copy-done.2
  2.5 0.9 copy-done.3
  3.4 0.9 copy-done.4
  4.3 78.5 %gather_rows.1 = (bf16[32,128,128]{2,1,0:T(8,128)(2,1)}, bf16[32,128,128]{2,1,0:T(8,128)(2,1)S(1)}, bf16[32,128,256]{2,1,0:T(8,128)(2,1)}, bf16[32,256,128]{2,1,...) custom-call(bf16[32,16,128]{2,1,0:T(8,128)(2,1)S(1)} %copy-done.3, ...), custom_call_target="tpu_custom_call" | custom-call | tf_op jit(solution)/shard_map/gather_rows/pallas_call | solution.py:290
  82.8 0.0 copy-start
  82.8 0.0 copy-start.7
  82.9 3.1 %fusion.13 = f32[32,256,128]{2,1,0:T(8,128)S(1)} fusion(bf16[32,128,256]{2,1,0:T(8,128)(2,1)} %get-tuple-element.18, bf16[128,32,128]{2,1,0:T(8,128)(2,1)} %get-tuple-element.15), kind=kOutput, calls=%fused_computation.22 | convolution fusion | flops 268435456 | bytes 7340032 | tf_op jit(solution)/shard_map/bjt,jbk->tjk/dot_general | solution.py:662
  86.0 0.0 copy-done.7
  86.0 1.9 fusion.18
  87.9 3.9 %fusion.6 = bf16[128,32,256]{0,2,1:T(8,128)(2,1)S(1)} fusion(f32[32,256,128]{2,1,0:T(8,128)S(1)} %fusion.13, bf16[32,256,128]{2,1,0:T(8,128)(2,1)S(1)} %copy-done.7, bf16[128,32,128]{2,1,0:T(8,128)(2,1)S(1)} %get-tuple-element.17), kind=kOutput, calls=%fused_computation.8 | convolution fusion | flops 289406976 | bytes 9437184 | tf_op jit(solution)/shard_map/jbt,bij->tbi/dot_general | solution.py:664
  91.9 3.1 %convolution_convert_fusion.refs_1_ = bf16[32,256,128]{2,1,0:T(8,128)(2,1)} fusion(bf16[128,32,128]{2,1,0:T(8,128)(2,1)S(1)} %get-tuple-element.17, f32[32,256,128]{2,1,0:T(8,128)S(1)} %fusion.13), kind=kOutput, calls=%fused_computation.18 | convolution fusion | flops 278921216 | bytes 7340032 | tf_op jit(solution)/shard_map/tbi,jbt->bij/dot_general | solution.py:673
  95.0 0.0 copy-done.5
  95.0 0.7 fusion.21
  95.7 0.5 copy-done.6
  96.2 2.1 convolution_convert_fusion.1.refs_0_
  98.2 2.7 %fusion.11 = (bf16[128,32,128]{2,1,0:T(8,128)(2,1)}, bf16[128,32,128]{2,1,0:T(8,128)(2,1)}) fusion(bf16[32,128,128]{2,1,0:T(8,128)(2,1)S(1)} %fusion.18, bf16[32,128,128]{2,1,0:T(8,128)(2,1)S(1)} %fusion.21), kind=kLoop, calls=%fused_computation.20 | loop fusion | bytes 4194304 | tf_op jit(solution)/shard_map/convert_element_type | solution.py:669
  100.9 109.6 %reduce_rows.1 = (bf16[128,4096]{1,0:T(8,128)(2,1)S(1)}, bf16[32,128,128]{2,1,0:T(8,128)(2,1)S(1)}, bf16[32,128,128]{2,1,0:T(8,128)(2,1)}, f32[32,16,256]{2,1,0:T(8,128)S(1)}, f32[32,32,128]{2,1,0:T(8,128)S(1)}) custom-call(bf16[32,128,256]{2,1,0:T(8,128)(2,1)} %convolution_convert_fusion.1.refs_0_, bf16[32,256,128]{2,1,0:T(8,128)(2,1)} %convolution_convert_fusion.refs_1_, ...), custom_call_target="tpu_custom_call" | custom-call | tf_op jit(solution)/shard_map/reduce_rows/pallas_call | solution.py:544
  210.6 2.8 %convert_element_type.36 = f32[32,128,128]{2,1,0:T(8,128)} convert(bf16[32,128,128]{2,1,0:T(8,128)(2,1)} %get-tuple-element.21) | non-fusion elementwise | flops 524288 | bytes 3145728 | tf_op jit(solution)/shard_map/convert_element_type | solution.py:688
  213.4 1.6 convert_element_type.37
  214.9 1.0 copy.44
  215.9 0.8 copy.45
  216.7 0.8 copy.46
  (6 shorter events, 0.0 us)
Async XLA Ops:
  0.6 1.0 copy-start.1
  1.6 0.9 copy-start.2
  2.5 0.9 copy-start.3
  3.4 0.9 copy-start.4
  82.8 5.1 %copy-start = (bf16[32,128,128]{2,1,0:T(8,128)(2,1)}, bf16[32,128,128]{2,1,0:T(8,128)(2,1)S(1)}, u32[]{:S(2)}) copy-start(bf16[32,128,128]{2,1,0:T(8,128)(2,1)S(1)} %get-tuple-element.19.refs_6_) | copy-start | bytes 3145732
  82.8 3.1 %copy-start.7 = (bf16[32,256,128]{2,1,0:T(8,128)(2,1)S(1)}, bf16[32,256,128]{2,1,0:T(8,128)(2,1)}, u32[]{:S(2)}) copy-start(bf16[32,256,128]{2,1,0:T(8,128)(2,1)} %get-tuple-element.16) | copy-start | bytes 6291460
  91.8 3.1 %copy-start.5 = (bf16[32,128,256]{2,1,0:T(8,128)(2,1)S(1)}, bf16[32,128,256]{2,1,0:T(8,128)(2,1)}, u32[]{:S(2)}) copy-start(bf16[32,128,256]{2,1,0:T(8,128)(2,1)} %get-tuple-element.18) | copy-start | bytes 6291460
  95.0 1.2 copy-start.6

commit v5 on v4

--- a/solution.py
+++ b/solution.py
@@ -494,7 +494,7 @@
     down.begin()
     up.begin()
     far = range(place.depth - 1, 1, -1)
-    for distance in far:
+    for distance in range(place.depth - 1, 0, -1):
         for reduce in reduces[shared:]:
             reduce.send_across(distance)
     pending = [make_ds, make_uf]
@@ -505,17 +505,16 @@
             pending.pop(0)()
     for make in pending:
         make()
-    for distance in (1, 0):
-        for reduce in reduces[shared:]:
-            reduce.send_across(distance)
+    for reduce in reduces[shared:]:
+        reduce.send_across(0)
+    for reduce in reduces[shared:]:
+        reduce.step(1)
     for distance in range(place.depth - 1, 0, -1):
         for reduce in reduces[:shared]:
             reduce.step(distance)
     for a in range(shared):
         reduces[a].last()
         gathers[a].begin()
-    for reduce in reduces[shared:]:
-        reduce.step(1)
     gathers[0].begin_wide()
     for gather in gathers:
         gather.step(1)

time: 218 us -> 209 us (0.959)
  Pallas kernels: 188 us -> 180 us
    pallas_call x1, Pallas kernels: 110 us -> 101 us  [reduce_rows(): pl.pallas_call(functools.partial(reduce_kernel, size, scale), out_shape=(...]
where the time goes in v5:
time: 209 us
  Pallas kernels  180 us (86%)
  matrix products  14.8 us (7%)
  local copies, waits for them, and re-layouts  9.46 us (5%)
  other arithmetic  4.35 us (2%)
    pallas_call x1, Pallas kernels, reduce_rows(): pl.pallas_call(functools.partial(reduce_kernel, size, scale), out_shape=(...  101 us
    pallas_call x1, Pallas kernels, gather_rows(): pl.pallas_call(functools.partial(gather_kernel, size), out_shape=tuple((j...  78.5 us
    unnamed x19, local copies, waits for them, and re-layouts  6.79 us

profile of v5, /device:TPU:0, one launch (start us, length us, event | category | flops | bytes accessed | tf_op | source)
XLA Modules:
  0.0 209.0 jit_solution(16563256063415125826)
XLA Ops:
  0.6 0.0 copy-start.1
  0.6 0.9 copy-done.1
  1.6 0.9 copy-done.2
  2.5 0.9 copy-done.3
  3.4 0.9 copy-done.4
  4.3 78.5 %gather_rows.1 = (bf16[32,128,128]{2,1,0:T(8,128)(2,1)}, bf16[32,128,128]{2,1,0:T(8,128)(2,1)S(1)}, bf16[32,128,256]{2,1,0:T(8,128)(2,1)}, bf16[32,256,128]{2,1,...) custom-call(bf16[32,16,128]{2,1,0:T(8,128)(2,1)S(1)} %copy-done.3, ...), custom_call_target="tpu_custom_call" | custom-call | tf_op jit(solution)/shard_map/gather_rows/pallas_call | solution.py:290
  82.8 0.0 copy-start
  82.8 0.0 copy-start.7
  82.9 3.1 %fusion.13 = f32[32,256,128]{2,1,0:T(8,128)S(1)} fusion(bf16[32,128,256]{2,1,0:T(8,128)(2,1)} %get-tuple-element.18, bf16[128,32,128]{2,1,0:T(8,128)(2,1)} %get-tuple-element.15), kind=kOutput, calls=%fused_computation.22 | convolution fusion | flops 268435456 | bytes 7340032 | tf_op jit(solution)/shard_map/bjt,jbk->tjk/dot_general | solution.py:661
  86.0 0.0 copy-done.7
  86.0 1.9 fusion.18
  87.9 0.0 copy-done
  87.9 3.9 %fusion.6 = bf16[128,32,256]{0,2,1:T(8,128)(2,1)S(1)} fusion(f32[32,256,128]{2,1,0:T(8,128)S(1)} %fusion.13, bf16[32,256,128]{2,1,0:T(8,128)(2,1)S(1)} %copy-done.7, bf16[128,32,128]{2,1,0:T(8,128)(2,1)S(1)} %get-tuple-element.17), kind=kOutput, calls=%fused_computation.8 | convolution fusion | flops 289406976 | bytes 9437184 | tf_op jit(solution)/shard_map/jbt,bij->tbi/dot_general | solution.py:663
  91.9 3.1 %convolution_convert_fusion.refs_1_ = bf16[32,256,128]{2,1,0:T(8,128)(2,1)} fusion(bf16[128,32,128]{2,1,0:T(8,128)(2,1)S(1)} %get-tuple-element.17, f32[32,256,128]{2,1,0:T(8,128)S(1)} %fusion.13), kind=kOutput, calls=%fused_computation.18 | convolution fusion | flops 278921216 | bytes 7340032 | tf_op jit(solution)/shard_map/tbi,jbt->bij/dot_general | solution.py:672
  95.0 0.7 fusion.21
  95.7 0.5 copy-done.6
  96.2 2.1 convolution_convert_fusion.1.refs_0_
  98.2 2.7 %fusion.11 = (bf16[128,32,128]{2,1,0:T(8,128)(2,1)}, bf16[128,32,128]{2,1,0:T(8,128)(2,1)}) fusion(bf16[32,128,128]{2,1,0:T(8,128)(2,1)S(1)} %fusion.18, bf16[32,128,128]{2,1,0:T(8,128)(2,1)S(1)} %fusion.21), kind=kLoop, calls=%fused_computation.20 | loop fusion | bytes 4194304 | tf_op jit(solution)/shard_map/convert_element_type | solution.py:668
  100.9 101.1 %reduce_rows.1 = (bf16[128,4096]{1,0:T(8,128)(2,1)S(1)}, bf16[32,128,128]{2,1,0:T(8,128)(2,1)S(1)}, bf16[32,128,128]{2,1,0:T(8,128)(2,1)}, f32[32,16,256]{2,1,0:T(8,128)S(1)}, f32[32,32,128]{2,1,0:T(8,128)S(1)}) custom-call(bf16[32,128,256]{2,1,0:T(8,128)(2,1)} %convolution_convert_fusion.1.refs_0_, bf16[32,256,128]{2,1,0:T(8,128)(2,1)} %convolution_convert_fusion.refs_1_, ...), custom_call_target="tpu_custom_call" | custom-call | tf_op jit(solution)/shard_map/reduce_rows/pallas_call | solution.py:543
  202.1 2.8 %convert_element_type.36 = f32[32,128,128]{2,1,0:T(8,128)} convert(bf16[32,128,128]{2,1,0:T(8,128)(2,1)} %get-tuple-element.21) | non-fusion elementwise | flops 524288 | bytes 3145728 | tf_op jit(solution)/shard_map/convert_element_type | solution.py:687
  204.8 1.6 convert_element_type.37
  206.4 1.0 copy.44
  207.4 0.8 copy.45
  208.2 0.8 copy.46
  (6 shorter events, 0.0 us)
Async XLA Ops:
  0.6 1.0 copy-start.1
  1.6 0.9 copy-start.2
  2.5 0.9 copy-start.3
  3.4 0.9 copy-start.4
  82.8 5.1 %copy-start = (bf16[32,128,128]{2,1,0:T(8,128)(2,1)}, bf16[32,128,128]{2,1,0:T(8,128)(2,1)S(1)}, u32[]{:S(2)}) copy-start(bf16[32,128,128]{2,1,0:T(8,128)(2,1)S(1)} %get-tuple-element.19.refs_6_) | copy-start | bytes 3145732
  82.8 3.1 %copy-start.7 = (bf16[32,256,128]{2,1,0:T(8,128)(2,1)S(1)}, bf16[32,256,128]{2,1,0:T(8,128)(2,1)}, u32[]{:S(2)}) copy-start(bf16[32,256,128]{2,1,0:T(8,128)(2,1)} %get-tuple-element.16) | copy-start | bytes 6291460
  91.8 3.1 %copy-start.5 = (bf16[32,128,256]{2,1,0:T(8,128)(2,1)S(1)}, bf16[32,128,256]{2,1,0:T(8,128)(2,1)}, u32[]{:S(2)}) copy-start(bf16[32,128,256]{2,1,0:T(8,128)(2,1)} %get-tuple-element.18) | copy-start | bytes 6291460
  95.0 1.2 copy-start.6
